TPU v7x, 32 devices: a whole 2x2x4 slice. The times are simulated.
32 devices in a mesh: chan: 4 (over z), sec: 8 (over y, x, core).
Axes of the slice: x: 2, y: 2, z: 4, core: 2. Of those that a mesh axis runs over, the one named last changes fastest.
Arguments:
- psi: bfloat16 [192, 4, 256, 256], P('sec'), may hold values from -6 to 6
- mpo: float32 [4, 4, 4], P('chan'), may hold values from -1.5 to 1.5
- left_env: bfloat16 [4, 64, 256, 256], P('chan', 'sec'), may hold values from -0.375 to 0.375
- right_env: bfloat16 [4, 192, 256, 256], P('chan', 'sec'), may hold values from -0.375 to 0.375
- left_dims: int32 [64], P('sec'), may hold values from 128 to 256, as said below
- right_dims: int32 [192], P('sec'), may hold values from 128 to 256, as said below
- dest_owner: int32 [192, 1], P('sec'), may hold values from 0 to 7, as said below
- left_slot: int32 [192], P('sec'), may hold values from 0 to 7
Outputs:
- h_psi: bfloat16 [192, 4, 256, 256], P('sec', None, 'chan')
Inputs may be any that keep to these rules, and one draw needn't show every extreme that they name: `dest_owner`: each device's 24 blocks name one owner at most 3 times; in every draw some owner is named exactly 3 times by the blocks of every device. `left_dims`: multiples of 128; both bounds are reached. `right_dims`: multiples of 128; both bounds are reached.
All inputs are finite; a program needn't handle non-finite values.
Results may differ from a plain program's by a relative error of at most 0.014.
Values may be sent and summed in bfloat16 or wider, within the bound.
No kernel may reach another device: no remote copies, remote signals or barrier semaphores. Data moves between devices by JAX's collectives and lax.ppermute only.
A program may use at most 192 MiB of HBM per device.

v0:
```python
import functools

import jax
import jax.numpy as jnp
from jax import lax
from jax.experimental import pallas as pl
from jax.experimental.pallas import tpu as pltpu
from jax.sharding import PartitionSpec as P

ANY = pl.BlockSpec(memory_space=pl.ANY)
SMEM = pl.BlockSpec(memory_space=pltpu.SMEM)


def after(x, *others):
    return lax.optimization_barrier((x, others))[0]


def digits(c, parity, hi, lo):
    return (c // lo, c % lo) if parity == 0 else (c % hi, c // hi)


def rank(h, l, parity, hi, lo):
    return h * lo + l if parity == 0 else l * hi + h


def left_kernel(hi, lo, where, own_dims, side_dims, own_left, side_left, *outs):
    own = outs[0].shape[1] // lo
    sectors, each = own_dims.shape[0], own_left.shape[0]
    step = pl.program_id(0)
    here, odd = where[0], where[1] == 1
    h = jnp.where(odd, here % hi, here // lo)
    l = jnp.where(odd, here // hi, here % lo)

    def fill(left, dims, at):
        for n in range(each):
            r = dims[at * each + n]
            for i in range(hi):
                for j in range(lo):
                    hh, ll = (h + i) % hi, (l + j) % lo
                    start = pl.multiple_of(jnp.where(odd, ll * hi + hh, hh * lo + ll) * own, own)
                    piece = left[n, pl.ds(start, own), :]
                    inside = (lax.broadcasted_iota(jnp.int32, piece.shape, 0) + start < r) & (
                        lax.broadcasted_iota(jnp.int32, piece.shape, 1) < r
                    )
                    outs[i][n, j * own : (j + 1) * own] = jnp.where(
                        inside, piece, jnp.zeros_like(piece)
                    )

    half = sectors // each

    @pl.when(step < half)
    def _():
        fill(own_left, own_dims, step)

    @pl.when(step >= half)
    def _():
        fill(side_left, side_dims, step - half)


def left_call(hi, lo, own_rows, where, own_dims, side_dims, own_left, side_left):
    sectors, width = own_left.shape[:2]
    each = 4 if sectors % 4 == 0 else 1
    half = sectors // each
    block = (each, lo * own_rows, width)
    return pl.pallas_call(
        functools.partial(left_kernel, hi, lo),
        grid_spec=pltpu.PrefetchScalarGridSpec(
            num_scalar_prefetch=3,
            grid=(2 * half,),
            in_specs=[
                pl.BlockSpec((each, width, width), lambda s, *_: (jnp.minimum(s, half - 1), 0, 0)),
                pl.BlockSpec((each, width, width), lambda s, *_: (jnp.maximum(s - half, 0), 0, 0)),
            ],
            out_specs=[pl.BlockSpec(block, lambda s, *_: (s, 0, 0))] * hi,
        ),
        out_shape=[jax.ShapeDtypeStruct((2 * sectors,) + block[1:], own_left.dtype)] * hi,
        compiler_params=pltpu.CompilerParams(vmem_limit_bytes=32 * 2**20),
        cost_estimate=pl.CostEstimate(
            flops=2 * own_left.size, bytes_accessed=8 * own_left.size, transcendentals=0
        ),
    )(where, own_dims, side_dims, own_left, side_left)


def plan_kernel(half, sectors, slots, me, dims, table, order, near, row, asked, most, seen):
    blocks = dims.shape[0]
    n_sec = table.shape[0]
    chips = n_sec // 2
    mine, parity = me[0] // 2, me[0] % 2

    def local(want):
        owner = want // sectors
        return ((owner % 2) ^ parity) * sectors + want % sectors

    def place(keep_wide):
        def body(k, at):
            fits = (dims[k] > half) == keep_wide

            @pl.when(fits)
            def _():
                order[at] = k

            return at + fits.astype(jnp.int32)

        return body

    wide = lax.fori_loop(0, blocks, place(True), jnp.int32(0))
    lax.fori_loop(0, blocks, place(False), wide)

    largest = table[0, blocks]
    for s in range(1, n_sec):
        largest = jnp.maximum(largest, table[s, blocks])
    most[0] = largest

    for chip in range(chips):
        seen[chip] = 0

    def source(k, _):
        want = table[me[0], k]
        chip = want // sectors // 2
        here = chip == mine
        count = seen[chip]
        seen[chip] = count + 1
        near[k] = here.astype(jnp.int32)
        far = ((chip ^ mine) - 1) * slots + jnp.minimum(count, slots - 1)
        row[k] = jnp.where(here, local(want), far)
        return 0

    lax.fori_loop(0, blocks, source, 0)

    for gap in range(1, chips):
        base = (gap - 1) * slots
        for n in range(slots):
            asked[base + n] = 0
        dest = (mine ^ gap) * 2 + parity

        def wish(k, count):
            want = table[dest, k]
            here = want // sectors // 2 == mine

            @pl.when(here)
            def _():
                asked[base + jnp.minimum(count, slots - 1)] = local(want)

            return count + here.astype(jnp.int32)

        lax.fori_loop(0, blocks, wish, jnp.int32(0))


def plan_call(half, sectors, slots, me, dims, table):
    blocks, chips = dims.shape[0], table.shape[0] // 2
    ints = [blocks, blocks, blocks, max(chips - 1, 1) * slots, 1]
    return pl.pallas_call(
        functools.partial(plan_kernel, half, sectors, slots),
        in_specs=[SMEM] * 3,
        out_specs=[SMEM] * 5,
        out_shape=[jax.ShapeDtypeStruct((n,), jnp.int32) for n in ints],
        scratch_shapes=[pltpu.SMEM((chips,), jnp.int32)],
        cost_estimate=pl.CostEstimate(flops=0, bytes_accessed=4 * table.size, transcendentals=0),
    )(me, dims, table)


def block_kernel(hi, rows, narrow, first, order, right_dims, near, row, mpo, psi, *refs):
    lefts, rights = refs[: 2 * hi], refs[2 * hi : 3 * hi]
    keep, send = refs[3 * hi :]
    states = psi.shape[1]
    k = order[pl.program_id(0) + first]
    is_near = jnp.full(lefts[0].shape[1:], near[k], jnp.int32) > 0
    stacked = jnp.concatenate(
        [jnp.where(is_near, lefts[2 * i][0], lefts[2 * i + 1][0]) for i in range(hi)], axis=0
    )
    parts = [
        jnp.dot(stacked, psi[0, p], preferred_element_type=jnp.float32) for p in range(states)
    ]
    total = None
    for i in range(hi):
        right = rights[i][0]
        if not narrow:
            r = right_dims[k]
            inside = (lax.broadcasted_iota(jnp.int32, right.shape, 0) < r) & (
                lax.broadcasted_iota(jnp.int32, right.shape, 1) < r
            )
            right = jnp.where(inside, right, jnp.zeros_like(right))
        mixed = []
        for s in range(states):
            acc = None
            for p in range(states):
                piece = parts[p][i * rows : (i + 1) * rows] * mpo[i, s * states + p]
                acc = piece if acc is None else acc + piece
            mixed.append(acc.astype(jnp.bfloat16))
        mixed = jnp.concatenate(mixed, axis=0)
        product = lax.dot_general(
            mixed, right, (((1,), (1,)), ((), ())), preferred_element_type=jnp.float32
        )
        total = product if total is None else total + product
    own = keep.shape[2]
    for s in range(states):
        keep[0, s] = total[s * rows : s * rows + own].astype(keep.dtype)
        for j in range(send.shape[0]):
            at = s * rows + (j + 1) * own
            send[j, 0, s] = total[at : at + own].astype(send.dtype)


def blocks_call(hi, lo, own_rows, narrow, span, base, scalars, mpo, psi, lefts, right, others):
    states, width = psi.shape[1], psi.shape[2]
    first, count = span.start, span.stop - span.start
    across = width // 2 if narrow else width
    rows = lo * own_rows

    def by_block(k, order, *_):
        return (order[k + first], 0, 0)

    def by_row(far):
        def index(k, order, right_dims, near, row, *_):
            block = order[k + first]
            return (jnp.where(near[block] == 1 - far, row[block], 0), 0, 0)

        return index

    grid_spec = pltpu.PrefetchScalarGridSpec(
        num_scalar_prefetch=5,
        grid=(count,),
        in_specs=[
            pl.BlockSpec((1, states, width, across), lambda *at: by_block(*at) + (0,)),
        ]
        + [pl.BlockSpec((1, rows, width), by_row(far)) for _ in range(hi) for far in range(2)]
        + [pl.BlockSpec((1, across, across), by_block)]
        + [pl.BlockSpec((1, across, across), lambda k, *_: (k + first - base, 0, 0))] * (hi - 1),
        out_specs=[
            pl.BlockSpec((1, states, own_rows, across), lambda k, *_: (k, 0, 0, 0)),
            pl.BlockSpec((lo - 1, 1, states, own_rows, across), lambda k, *_: (0, k, 0, 0, 0)),
        ],
    )
    return pl.pallas_call(
        functools.partial(block_kernel, hi, rows, narrow, first),
        grid_spec=grid_spec,
        out_shape=[
            jax.ShapeDtypeStruct((count, states, own_rows, across), jnp.bfloat16),
            jax.ShapeDtypeStruct((lo - 1, count, states, own_rows, across), jnp.bfloat16),
        ],
        compiler_params=pltpu.CompilerParams(vmem_limit_bytes=40 * 2**20),
        cost_estimate=pl.CostEstimate(
            flops=count * 2 * hi * rows * states * across * (width + across),
            bytes_accessed=count * 5 * states * width * across,
            transcendentals=0,
        ),
    )(*scalars, mpo, psi, *lefts, right, *others)


def add_kernel(terms, span, order, *refs):
    out, total, sems = refs[-3:]
    across = refs[0].shape[-1]
    copies = []
    for k in range(span.stop - span.start):
        acc = refs[0][k].astype(jnp.float32)
        for j in range(1, terms):
            acc = acc + refs[j][k].astype(jnp.float32)
        total[k, :, :, :across] = acc.astype(total.dtype)
        if across < total.shape[-1]:
            total[k, :, :, across:] = jnp.zeros(acc.shape[:-1] + (total.shape[-1] - across,), total.dtype)
        copy = pltpu.make_async_copy(total.at[k], out.at[order[k + span.start]], sems.at[k])
        copy.start()
        copies.append(copy)
    for copy in copies:
        copy.wait()


def add_call(shape, span, order, terms, out):
    count = span.stop - span.start
    return pl.pallas_call(
        functools.partial(add_kernel, len(terms), span),
        in_specs=[SMEM]
        + [pl.BlockSpec(memory_space=pltpu.VMEM)] * len(terms)
        + ([] if out is None else [ANY]),
        out_specs=ANY,
        out_shape=jax.ShapeDtypeStruct(shape, jnp.bfloat16),
        scratch_shapes=[
            pltpu.VMEM((count,) + shape[1:], jnp.bfloat16),
            pltpu.SemaphoreType.DMA((count,)),
        ],
        input_output_aliases={} if out is None else {1 + len(terms): 0},
        compiler_params=pltpu.CompilerParams(vmem_limit_bytes=24 * 2**20),
        cost_estimate=pl.CostEstimate(
            flops=terms[0].size, bytes_accessed=6 * terms[0].size, transcendentals=0
        ),
    )(order, *terms, *([] if out is None else [out]))


def on_device(n_chan, n_sec, psi, mpo, left_env, right_env, left_dims, right_dims, dest_owner, left_slot):
    blocks, states, width = psi.shape[:3]
    sectors = left_env.shape[1]
    half = width // 2
    hi = 2 if n_chan % 2 == 0 else 1
    lo = n_chan // hi
    own_rows = width // n_chan
    here, me = lax.axis_index("chan"), lax.axis_index("sec")
    odd = me % 2
    right = right_env[0]
    step = max(blocks // 6, 1)

    def route(x, up, along):
        pairs = []
        for c in range(n_chan):
            for s in range(n_sec):
                h, l = digits(c, s % 2, hi, lo)
                to = rank((h + up) % hi, (l + along) % lo, s % 2, hi, lo)
                pairs.append((c * n_sec + s, to * n_sec + s))
        return lax.ppermute(x, ("chan", "sec"), pairs)

    def to_partners(x):
        return [route(x, i, 0) for i in range(1, hi)]

    def beside(x):
        return lax.ppermute(x, "sec", [(s, s ^ 1) for s in range(n_sec)])

    def packs(x, asked):
        return [
            jnp.take(x, asked[(gap - 1) * slots : gap * slots], axis=0, mode="clip")
            for gap in range(1, n_sec // 2)
        ]

    def over_chips(packed):
        parts = []
        for gap, x in enumerate(packed, 1):
            parts.append(lax.ppermute(x, "sec", [(s, s ^ (2 * gap)) for s in range(n_sec)]))
        return jnp.concatenate(parts)

    side_left, side_dims = beside(left_env[0]), beside(left_dims)
    slots = 2 * -(-blocks // n_sec)
    wants = dest_owner[:, 0] * sectors + left_slot
    n_wide = jnp.sum((right_dims > half).astype(jnp.int32))[None]
    mine = jnp.arange(n_sec, dtype=jnp.int32)[:, None] == me
    table = lax.psum(jnp.where(mine, jnp.concatenate([wants, n_wide])[None], 0), "sec")
    order, near, row, asked, most = plan_call(half, sectors, slots, me[None], right_dims, table)
    most_wide = most[0]
    shards = left_call(
        hi, lo, own_rows, jnp.stack([here, odd]).astype(jnp.int32),
        left_dims, side_dims, left_env[0], side_left,
    )
    swapped = [route(shards[i], i, 0) for i in range(1, hi)]
    mpo_own = after(mpo[0], order)
    mpo_all = jnp.stack([mpo_own] + to_partners(mpo_own)).reshape(hi, states * states)
    scalars = (order, right_dims, near, row)
    caps = sorted({max(2, blocks * q // 12) for q in (7, 8, 9)} | {blocks})
    first = after(jnp.take(right, order[: caps[0]], axis=0, mode="clip"), swapped)

    def run(cap, scalars, asked, shards, swapped, first, mpo_all):
        order = scalars[0]
        moved = [to_partners(first)]
        sources = [shards[0]] + swapped
        packed = [packs(x, asked) for x in sources]
        bounds = [(0, caps[0])]
        if cap > caps[0]:
            bounds.append((caps[0], cap))
            more = jnp.take(right, order[caps[0] : cap], axis=0, mode="clip")
            moved.append(to_partners(after(more, packed)))
        spans = []
        for n, (low, high) in enumerate(bounds):
            for a in range(low, high, step):
                spans.append((slice(a, min(a + step, high)), False, low, n))
        rest = blocks - cap
        count = -(-rest // (step + 1))
        for q in range(count):
            span = slice(cap + rest * q // count, cap + rest * (q + 1) // count)
            spans.append((span, True, cap, len(moved)))
        if rest:
            thin = jnp.take(right, order[cap:], axis=0, mode="clip")[:, :half, :half]
            moved.append(to_partners(after(thin, packed)))
        total = len(spans)
        lefts = []
        for x, parts in zip(sources, packed):
            lefts += [x, over_chips(parts)]
        shape = (blocks, states, own_rows, width)
        out, terms = None, []
        for span, narrow, base, n in spans:
            keep, send = blocks_call(
                hi, lo, own_rows, narrow, span, base, scalars, mpo_all, psi, lefts, right, moved[n]
            )
            mpo_all = after(mpo_all, keep, *([] if terms else moved[1:]))
            terms.append([keep] + [route(send[j - 1], 0, j) for j in range(1, lo)])
        terms[0][0] = after(terms[0][0], terms[-1][0])
        for m in range(total):
            out = add_call(shape, spans[m][0], order, terms[m], out)
        return out

    which = sum((most_wide > cap).astype(jnp.int32) for cap in caps[:-1])
    return lax.switch(
        which, [functools.partial(run, cap) for cap in caps], scalars, asked,
        shards, swapped, first, mpo_all,
    )


def solution(mesh):
    in_specs = (
        P("sec", None, None, None),
        P("chan", None, None),
        P("chan", "sec", None, None),
        P("chan", "sec", None, None),
        P("sec"),
        P("sec"),
        P("sec", None),
        P("sec"),
    )
    out_specs = P("sec", None, "chan", None)
    return jax.shard_map(
        functools.partial(on_device, mesh.shape["chan"], mesh.shape["sec"]),
        mesh=mesh,
        in_specs=in_specs,
        out_specs=out_specs,
        check_vma=False,
    )
```

profile of v0, /device:TPU:0, one launch (start us, length us, event | category | flops | bytes accessed | tf_op | source)
XLA Modules:
  0.0 149.6 jit_solution(16479873217155358353)
XLA Ops:
  0.7 2.3 %collective-permute-done.61.side_dims = s32[8]{0:T(128)S(1)} collective-permute-done((s32[8]{0:T(128)}, s32[8]{0:T(128)S(1)}, u32[]{:S(2)}, u32[]{:S(2)}) %collective-permute-start.61) | collective-permute-done | bytes 64 | tf_op jit(solution)/shard_map/ppermute | solution.py:313
  6.5 4.0 %collective-permute-start.63 = (bf16[16,128,256]{2,1,0:T(8,128)(2,1)S(1)}, bf16[16,128,256]{2,1,0:T(8,128)(2,1)}, u32[]{:S(2)}, u32[]{:S(2)}) collective-permute-start(bf16[16,128,256]{2,1,0:T(8,128)(2,1)S(1)} %get-tuple-element.241), channel_id=1, source_target_pairs={{0,16},{1,9},{2,18},{3,11},{4,20},{5,13},{6,22},{7,15},{8,24},{9,1... | collective-permute-start | bytes 3145736 | tf_op jit(solution)/shard_map/ppermute | solution.py:307
  11.9 8.6 %psum.7.table = s32[8,25]{1,0:T(8,128)} all-reduce(s32[8,25]{1,0:T(8,128)S(1)} %broadcast_select_fusion), channel_id=1, replica_groups=mesh['chan'=4,'sec'=8] {'sec'}, use_global_device_ids=true, to_apply=%region_1.2 | all-reduce | flops 200 | bytes 1600 | tf_op jit(solution)/shard_map/psum | solution.py:332
  20.5 4.1 %shard_map.86 = (s32[24]{0:T(128)S(1)}, s32[24]{0:T(128)S(1)}, s32[24]{0:T(128)S(1)}, s32[18]{0:T(128)S(1)}, s32[1]{0:T(128)}) custom-call(s32[1]{0:T(128)} %bitcast.27.me, s32[24]{0:T(128)S(1)} %copy-done.22, s32[8,25]{1,0:T(8,128)} %psum.7.table), custom_call_target="tpu_custom_call" | custom-call | bytes 800 | tf_op jit(solution)/shard_map/pallas_call | solution.py:152
  27.7 3.8 %gather_fusion.30 = bf16[14,256,256]{2,1,0:T(8,128)(2,1)} fusion(bf16[24,256,256]{2,1,0:T(8,128)(2,1)} %bitcast.79, s32[1024]{0:T(1024)S(1)} %pad_clamp_fusion.18), kind=kCustom, calls=%fused_computation.30 | custom fusion | bytes 3670072 | tf_op jit(solution)/shard_map/jit(_take)/gather | solution.py:344
  33.5 115.9 %conditional.1 = (bf16[24,4,64,256]{3,2,1,0:T(8,128)(2,1)}) conditional(s32[]{:T(128)} %bitcast.30, (s32[18]{0:T(128)S(1)}, bf16[16,128,256]{2,1,0:T(8,128)(2,1)S(1)}, bf16[16,128,256]{2,1,0:T(8,128)(2,1)}, bf16[14,256,256]{2,1,0:T(8,128)(2,1)}, s32[24]{0:T(128)S(1)}, /*index=5*/s32[24]{0:T(128)S(1)}, ...), branch_computations={%region_2.3_spmd, %region_3.4_spmd, %region_4.5_spmd, %region_5.6_... | conditional | flops 6444027904 | bytes 184042784 | solution.py:386
  33.7 2.5 %collective-permute-start.20 = (bf16[14,256,256]{2,1,0:T(8,128)(2,1)}, bf16[14,256,256]{2,1,0:T(8,128)(2,1)S(1)}, u32[]{:S(2)}, u32[]{:S(2)}) collective-permute-start(bf16[14,256,256]{2,1,0:T(8,128)(2,1)} %get-tuple-element.138), channel_id=1, source_target_pairs={{0,16},{1,9},{2,18},{3,11},{4,20},{5,13},{6,22},{7,15},{8,24},{9,1... | collective-permute-start | bytes 5505032 | tf_op jit(solution)/shard_map/cond/branch_1_fun/ppermute | solution.py:307
  36.3 2.6 %gather_fusion.10 = bf16[6,128,256]{2,1,0:T(8,128)(2,1)} fusion(bf16[16,128,256]{2,1,0:T(8,128)(2,1)} %get-tuple-element.136.refs_2_, s32[1024]{0:T(1024)S(1)} %pad_clamp_fusion.8), kind=kCustom, calls=%fused_computation.10 | custom fusion | bytes 786456 | tf_op jit(solution)/shard_map/cond/branch_1_fun/jit(_take)/gather | solution.py:317
  42.2 2.6 %gather_fusion.11 = bf16[6,128,256]{2,1,0:T(8,128)(2,1)} fusion(bf16[16,128,256]{2,1,0:T(8,128)(2,1)} %get-tuple-element.136.refs_2_, s32[1024]{0:T(1024)S(1)} %pad_clamp_fusion.7), kind=kCustom, calls=%fused_computation.11 | custom fusion | bytes 786456 | tf_op jit(solution)/shard_map/cond/branch_1_fun/jit(_take)/gather | solution.py:317
  46.4 2.5 %gather_fusion.12 = bf16[6,128,256]{2,1,0:T(8,128)(2,1)} fusion(bf16[16,128,256]{2,1,0:T(8,128)(2,1)} %get-tuple-element.136.refs_2_, s32[1024]{0:T(1024)S(1)} %pad_clamp_fusion.6), kind=kCustom, calls=%fused_computation.12 | custom fusion | bytes 786456 | tf_op jit(solution)/shard_map/cond/branch_1_fun/jit(_take)/gather | solution.py:317
  53.2 3.1 %gather_fusion.13 = bf16[2,256,256]{2,1,0:T(8,128)(2,1)} fusion(bf16[24,256,256]{2,1,0:T(8,128)(2,1)} %get-tuple-element.137.refs_4_, s32[1024]{0:T(1024)S(1)} %get-tuple-element.255), kind=kCustom, calls=%fused_computation.13 | custom fusion | bytes 524296 | tf_op jit(solution)/shard_map/cond/branch_1_fun/jit(_take)/gather | solution.py:354
  56.3 3.5 %gather_fusion.14 = bf16[8,256,256]{2,1,0:T(8,128)(2,1)} fusion(bf16[24,256,256]{2,1,0:T(8,128)(2,1)} %get-tuple-element.137.refs_4_, s32[1024]{0:T(1024)S(1)} %get-tuple-element.254), kind=kCustom, calls=%fused_computation.14 | custom fusion | bytes 2097184 | tf_op jit(solution)/shard_map/cond/branch_1_fun/jit(_take)/gather | solution.py:366
  67.2 2.7 %collective-permute-start.22 = (bf16[8,128,128]{2,1,0:T(8,128)(2,1)S(1)}, bf16[8,128,128]{2,1,0:T(8,128)(2,1)S(1)}, u32[]{:S(2)}, u32[]{:S(2)}) collective-permute-start(bf16[8,128,128]{2,1,0:T(8,128)(2,1)S(1)} %slice.142), channel_id=1, source_target_pairs={{0,16},{1,9},{2,18},{3,11},{4,20},{5,13},{6,22},{7,15},{8,24},{9,1... | collective-permute-start | bytes 786440 | tf_op jit(solution)/shard_map/cond/branch_1_fun/ppermute | solution.py:307
  70.0 11.2 %collective-permute-done.15 = bf16[6,128,256]{2,1,0:T(8,128)(2,1)S(1)} collective-permute-done((bf16[6,128,256]{2,1,0:T(8,128)(2,1)}, bf16[6,128,256]{2,1,0:T(8,128)(2,1)S(1)}, u32[]{:S(2)}, u32[]{:S(2)}) %collective-permute-start.15) | collective-permute-done | bytes 393248 | tf_op jit(solution)/shard_map/cond/branch_1_fun/ppermute | solution.py:324
  81.3 6.5 %branch_1_fun.14 = (bf16[4,4,64,256]{3,2,1,0:T(8,128)(2,1)S(1)}, bf16[1,4,4,64,256]{4,3,2,1,0:T(8,128)(2,1)S(1)}) custom-call(s32[24]{0:T(128)S(1)} %get-tuple-element.128.order, s32[24]{0:T(128)S(1)} %get-tuple-element.129.right_dims, s32[24]{0:T(128)S(1)} %get-tuple-element.130.near, s32[24]{0:T(128)S(1)} %get-tuple-element.131.row, ...), custom_call_target="tpu_custom_call" | custom-call | flops 1073741824 | bytes 5242880 | tf_op jit(solution)/shard_map/cond/branch_1_fun/pallas_call | solution.py:233
  90.5 4.6 %branch_1_fun.15 = (bf16[4,4,64,256]{3,2,1,0:T(8,128)(2,1)S(1)}, bf16[1,4,4,64,256]{4,3,2,1,0:T(8,128)(2,1)S(1)}) custom-call(s32[24]{0:T(128)S(1)} %get-tuple-element.128.order, s32[24]{0:T(128)S(1)} %get-tuple-element.129.right_dims, s32[24]{0:T(128)S(1)} %get-tuple-element.130.near, s32[24]{0:T(128)S(1)} %get-tuple-element.131.row, ...), custom_call_target="tpu_custom_call" | custom-call | flops 1073741824 | bytes 5242880 | tf_op jit(solution)/shard_map/cond/branch_1_fun/pallas_call | solution.py:233
  95.7 4.5 %branch_1_fun.16 = (bf16[4,4,64,256]{3,2,1,0:T(8,128)(2,1)S(1)}, bf16[1,4,4,64,256]{4,3,2,1,0:T(8,128)(2,1)S(1)}) custom-call(s32[24]{0:T(128)S(1)} %get-tuple-element.128.order, s32[24]{0:T(128)S(1)} %get-tuple-element.129.right_dims, s32[24]{0:T(128)S(1)} %get-tuple-element.130.near, s32[24]{0:T(128)S(1)} %get-tuple-element.131.row, ...), custom_call_target="tpu_custom_call" | custom-call | flops 1073741824 | bytes 5242880 | tf_op jit(solution)/shard_map/cond/branch_1_fun/pallas_call | solution.py:233
  101.7 3.0 %branch_1_fun.17 = (bf16[2,4,64,256]{3,2,1,0:T(8,128)(2,1)S(1)}, bf16[1,2,4,64,256]{4,3,2,1,0:T(8,128)(2,1)S(1)}) custom-call(s32[24]{0:T(128)S(1)} %get-tuple-element.128.order, s32[24]{0:T(128)S(1)} %get-tuple-element.129.right_dims, s32[24]{0:T(128)S(1)} %get-tuple-element.130.near, s32[24]{0:T(128)S(1)} %get-tuple-element.131.row, ...), custom_call_target="tpu_custom_call" | custom-call | flops 536870912 | bytes 2621440 | tf_op jit(solution)/shard_map/cond/branch_1_fun/pallas_call | solution.py:233
  104.8 3.4 %branch_1_fun.18 = (bf16[2,4,64,256]{3,2,1,0:T(8,128)(2,1)S(1)}, bf16[1,2,4,64,256]{4,3,2,1,0:T(8,128)(2,1)S(1)}) custom-call(s32[24]{0:T(128)S(1)} %get-tuple-element.128.order, s32[24]{0:T(128)S(1)} %get-tuple-element.129.right_dims, s32[24]{0:T(128)S(1)} %get-tuple-element.130.near, s32[24]{0:T(128)S(1)} %get-tuple-element.131.row, ...), custom_call_target="tpu_custom_call" | custom-call | flops 536870912 | bytes 2621440 | tf_op jit(solution)/shard_map/cond/branch_1_fun/pallas_call | solution.py:233
  110.3 4.5 %branch_1_fun.19 = (bf16[4,4,64,128]{3,2,1,0:T(8,128)(2,1)S(1)}, bf16[1,4,4,64,128]{4,3,2,1,0:T(8,128)(2,1)S(1)}) custom-call(s32[24]{0:T(128)S(1)} %get-tuple-element.128.order, s32[24]{0:T(128)S(1)} %get-tuple-element.129.right_dims, s32[24]{0:T(128)S(1)} %get-tuple-element.130.near, s32[24]{0:T(128)S(1)} %get-tuple-element.131.row, ...), custom_call_target="tpu_custom_call" | custom-call | flops 402653184 | bytes 2621440 | tf_op jit(solution)/shard_map/cond/branch_1_fun/pallas_call | solution.py:233
  114.8 4.4 %branch_1_fun.20 = (bf16[4,4,64,128]{3,2,1,0:T(8,128)(2,1)S(1)}, bf16[1,4,4,64,128]{4,3,2,1,0:T(8,128)(2,1)S(1)}) custom-call(s32[24]{0:T(128)S(1)} %get-tuple-element.128.order, s32[24]{0:T(128)S(1)} %get-tuple-element.129.right_dims, s32[24]{0:T(128)S(1)} %get-tuple-element.130.near, s32[24]{0:T(128)S(1)} %get-tuple-element.131.row, ...), custom_call_target="tpu_custom_call" | custom-call | flops 402653184 | bytes 2621440 | tf_op jit(solution)/shard_map/cond/branch_1_fun/pallas_call | solution.py:233
  126.6 9.8 %collective-permute-done.26.refs_1_ = bf16[2,4,64,256]{3,2,1,0:T(8,128)(2,1)S(1)} collective-permute-done((bf16[2,4,64,256]{3,2,1,0:T(8,128)(2,1)S(1)}, bf16[2,4,64,256]{3,2,1,0:T(8,128)(2,1)S(1)}, u32[]{:S(2)}, u32[]{:S(2)}) %collective-permute-start.26) | collective-permute-done | bytes 262176 | tf_op jit(solution)/shard_map/cond/branch_1_fun/ppermute | solution.py:307
  139.1 3.0 %collective-permute-done.24.refs_1_ = bf16[4,4,64,128]{3,2,1,0:T(8,128)(2,1)S(1)} collective-permute-done((bf16[4,4,64,128]{3,2,1,0:T(8,128)(2,1)S(1)}, bf16[4,4,64,128]{3,2,1,0:T(8,128)(2,1)S(1)}, u32[]{:S(2)}, u32[]{:S(2)}) %collective-permute-start.24) | collective-permute-done | bytes 262176 | tf_op jit(solution)/shard_map/cond/branch_1_fun/ppermute | solution.py:307
  143.5 4.0 %collective-permute-done.23.refs_1_ = bf16[4,4,64,128]{3,2,1,0:T(8,128)(2,1)S(1)} collective-permute-done((bf16[4,4,64,128]{3,2,1,0:T(8,128)(2,1)S(1)}, bf16[4,4,64,128]{3,2,1,0:T(8,128)(2,1)S(1)}, u32[]{:S(2)}, u32[]{:S(2)}) %collective-permute-start.23) | collective-permute-done | bytes 262176 | tf_op jit(solution)/shard_map/cond/branch_1_fun/ppermute | solution.py:307
  (100 shorter events, 45.0 us)
Async XLA Ops:
  0.0 11.1 %copy-start.34 = (s32[24,1]{0,1:T(1,128)S(1)}, s32[24,1]{0,1:T(1,128)}, u32[]{:S(2)}) copy-start(s32[24,1]{0,1:T(1,128)} %param.18) | copy-start | bytes 292
  0.0 24.7 %copy-start.32 = (f32[1,4,4]{2,1,0:T(4,128)S(1)}, f32[1,4,4]{2,1,0:T(4,128)}, u32[]{:S(2)}) copy-start(f32[1,4,4]{2,1,0:T(4,128)} %param.13) | copy-start | bytes 196
  0.0 3.0 %collective-permute-start.62 = (bf16[8,256,256]{2,1,0:T(8,128)(2,1)}, bf16[8,256,256]{2,1,0:T(8,128)(2,1)S(1)}, u32[]{:S(2)}, u32[]{:S(2)}) collective-permute-start(bf16[8,256,256]{2,1,0:T(8,128)(2,1)} %bitcast.38), channel_id=1, source_target_pairs={{0,1},{1,0},{2,3},{3,2},{4,5},{5,4},{6,7},{7,6},{8,9},{9,8},{10,11... | collective-permute-start | bytes 3145736 | tf_op jit(solution)/shard_map/ppermute | solution.py:313
  0.5 2.5 %collective-permute-start.61 = (s32[8]{0:T(128)}, s32[8]{0:T(128)S(1)}, u32[]{:S(2)}, u32[]{:S(2)}) collective-permute-start(s32[8]{0:T(128)} %own_dims.1), channel_id=1, source_target_pairs={{0,1},{1,0},{2,3},{3,2},{4,5},{5,4},{6,7},{7,6},{8,9},{9,8},{10,11... | collective-permute-start | bytes 104 | tf_op jit(solution)/shard_map/ppermute | solution.py:313
  6.5 27.0 %collective-permute-start.63 = (bf16[16,128,256]{2,1,0:T(8,128)(2,1)S(1)}, bf16[16,128,256]{2,1,0:T(8,128)(2,1)}, u32[]{:S(2)}, u32[]{:S(2)}) collective-permute-start(bf16[16,128,256]{2,1,0:T(8,128)(2,1)S(1)} %get-tuple-element.241), channel_id=1, source_target_pairs={{0,16},{1,9},{2,18},{3,11},{4,20},{5,13},{6,22},{7,15},{8,24},{9,1... | collective-permute-start | bytes 3145736 | tf_op jit(solution)/shard_map/ppermute | solution.py:307
  24.7 8.7 %collective-permute-start.64 = (f32[4,4]{1,0:T(4,128)S(1)}, f32[4,4]{1,0:T(4,128)S(1)}, u32[]{:S(2)}, u32[]{:S(2)}) collective-permute-start(f32[4,4]{1,0:T(4,128)S(1)} %bitcast.85), channel_id=1, source_target_pairs={{0,16},{1,9},{2,18},{3,11},{4,20},{5,13},{6,22},{7,15},{8,24},{9,1... | collective-permute-start | bytes 200 | tf_op jit(solution)/shard_map/ppermute | solution.py:307
  33.7 68.0 %copy-start.7 = (bf16[16,128,256]{2,1,0:T(8,128)(2,1)}, bf16[16,128,256]{2,1,0:T(8,128)(2,1)S(1)}, u32[]{:S(2)}) copy-start(bf16[16,128,256]{2,1,0:T(8,128)(2,1)S(1)} %get-tuple-element.134.refs_0_) | copy-start | bytes 3145732 | tf_op jit(solution)/shard_map/cond
  33.7 47.6 %collective-permute-start.20 = (bf16[14,256,256]{2,1,0:T(8,128)(2,1)}, bf16[14,256,256]{2,1,0:T(8,128)(2,1)S(1)}, u32[]{:S(2)}, u32[]{:S(2)}) collective-permute-start(bf16[14,256,256]{2,1,0:T(8,128)(2,1)} %get-tuple-element.138), channel_id=1, source_target_pairs={{0,16},{1,9},{2,18},{3,11},{4,20},{5,13},{6,22},{7,15},{8,24},{9,1... | collective-permute-start | bytes 5505032 | tf_op jit(solution)/shard_map/cond/branch_1_fun/ppermute | solution.py:307
  38.9 22.0 %collective-permute-start.17 = (bf16[6,128,256]{2,1,0:T(8,128)(2,1)}, bf16[6,128,256]{2,1,0:T(8,128)(2,1)}, u32[]{:S(2)}, u32[]{:S(2)}) collective-permute-start(bf16[6,128,256]{2,1,0:T(8,128)(2,1)} %gather_fusion.10), channel_id=1, source_target_pairs={{0,2},{1,3},{2,0},{3,1},{4,6},{5,7},{6,4},{7,5},{8,10},{9,11},{10,... | collective-permute-start | bytes 1179656 | tf_op jit(solution)/shard_map/cond/branch_1_fun/ppermute | solution.py:324
  41.7 21.8 %collective-permute-start.14 = (bf16[6,128,256]{2,1,0:T(8,128)(2,1)}, bf16[6,128,256]{2,1,0:T(8,128)(2,1)}, u32[]{:S(2)}, u32[]{:S(2)}) collective-permute-start(bf16[6,128,256]{2,1,0:T(8,128)(2,1)} %gather_fusion.7), channel_id=1, source_target_pairs={{0,2},{1,3},{2,0},{3,1},{4,6},{5,7},{6,4},{7,5},{8,10},{9,11},{10,... | collective-permute-start | bytes 1179656 | tf_op jit(solution)/shard_map/cond/branch_1_fun/ppermute | solution.py:324
  44.8 20.2 %collective-permute-start.18 = (bf16[6,128,256]{2,1,0:T(8,128)(2,1)}, bf16[6,128,256]{2,1,0:T(8,128)(2,1)}, u32[]{:S(2)}, u32[]{:S(2)}) collective-permute-start(bf16[6,128,256]{2,1,0:T(8,128)(2,1)} %gather_fusion.11), channel_id=1, source_target_pairs={{0,4},{1,5},{2,6},{3,7},{4,0},{5,1},{6,2},{7,3},{8,12},{9,13},{10,... | collective-permute-start | bytes 1179656 | tf_op jit(solution)/shard_map/cond/branch_1_fun/ppermute | solution.py:324
  48.9 18.3 %collective-permute-start.19 = (bf16[6,128,256]{2,1,0:T(8,128)(2,1)}, bf16[6,128,256]{2,1,0:T(8,128)(2,1)S(1)}, u32[]{:S(2)}, u32[]{:S(2)}) collective-permute-start(bf16[6,128,256]{2,1,0:T(8,128)(2,1)} %gather_fusion.12), channel_id=1, source_target_pairs={{0,6},{1,7},{2,4},{3,5},{4,2},{5,3},{6,0},{7,1},{8,14},{9,15},{10,... | collective-permute-start | bytes 1179656 | tf_op jit(solution)/shard_map/cond/branch_1_fun/ppermute | solution.py:324
  60.8 20.4 %collective-permute-start.15 = (bf16[6,128,256]{2,1,0:T(8,128)(2,1)}, bf16[6,128,256]{2,1,0:T(8,128)(2,1)S(1)}, u32[]{:S(2)}, u32[]{:S(2)}) collective-permute-start(bf16[6,128,256]{2,1,0:T(8,128)(2,1)} %gather_fusion.8), channel_id=1, source_target_pairs={{0,4},{1,5},{2,6},{3,7},{4,0},{5,1},{6,2},{7,3},{8,12},{9,13},{10,... | collective-permute-start | bytes 1179656 | tf_op jit(solution)/shard_map/cond/branch_1_fun/ppermute | solution.py:324
  63.5 17.8 %collective-permute-start.16 = (bf16[6,128,256]{2,1,0:T(8,128)(2,1)S(1)}, bf16[6,128,256]{2,1,0:T(8,128)(2,1)S(1)}, u32[]{:S(2)}, u32[]{:S(2)}) collective-permute-start(bf16[6,128,256]{2,1,0:T(8,128)(2,1)S(1)} %copy-done.25), channel_id=1, source_target_pairs={{0,6},{1,7},{2,4},{3,5},{4,2},{5,3},{6,0},{7,1},{8,14},{9,15},{10,... | collective-permute-start | bytes 1179656 | tf_op jit(solution)/shard_map/cond/branch_1_fun/ppermute | solution.py:324
  65.1 22.8 %collective-permute-start.21 = (bf16[2,256,256]{2,1,0:T(8,128)(2,1)S(1)}, bf16[2,256,256]{2,1,0:T(8,128)(2,1)S(1)}, u32[]{:S(2)}, u32[]{:S(2)}) collective-permute-start(bf16[2,256,256]{2,1,0:T(8,128)(2,1)S(1)} %copy-done.31), channel_id=1, source_target_pairs={{0,16},{1,9},{2,18},{3,11},{4,20},{5,13},{6,22},{7,15},{8,24},{9,1... | collective-permute-start | bytes 786440 | tf_op jit(solution)/shard_map/cond/branch_1_fun/ppermute | solution.py:307
  66.9 14.5 %copy-start.11 = (bf16[16,128,256]{2,1,0:T(8,128)(2,1)S(1)}, bf16[16,128,256]{2,1,0:T(8,128)(2,1)}, u32[]{:S(2)}) copy-start(bf16[16,128,256]{2,1,0:T(8,128)(2,1)} %get-tuple-element.136.refs_2_) | copy-start | bytes 3145732 | tf_op jit(solution)/shard_map/cond
  67.2 21.9 %collective-permute-start.22 = (bf16[8,128,128]{2,1,0:T(8,128)(2,1)S(1)}, bf16[8,128,128]{2,1,0:T(8,128)(2,1)S(1)}, u32[]{:S(2)}, u32[]{:S(2)}) collective-permute-start(bf16[8,128,128]{2,1,0:T(8,128)(2,1)S(1)} %slice.142), channel_id=1, source_target_pairs={{0,16},{1,9},{2,18},{3,11},{4,20},{5,13},{6,22},{7,15},{8,24},{9,1... | collective-permute-start | bytes 786440 | tf_op jit(solution)/shard_map/cond/branch_1_fun/ppermute | solution.py:307
  89.1 30.1 %collective-permute-start.29 = (bf16[4,4,64,256]{3,2,1,0:T(8,128)(2,1)S(1)}, bf16[4,4,64,256]{3,2,1,0:T(8,128)(2,1)S(1)}, u32[]{:S(2)}, u32[]{:S(2)}) collective-permute-start(bf16[4,4,64,256]{3,2,1,0:T(8,128)(2,1)S(1)} %bitcast.45), channel_id=1, source_target_pairs={{0,8},{1,17},{2,10},{3,19},{4,12},{5,21},{6,14},{7,23},{8,0},{9,25... | collective-permute-start | bytes 1572872 | tf_op jit(solution)/shard_map/cond/branch_1_fun/ppermute | solution.py:307
  95.0 24.8 %collective-permute-start.28 = (bf16[4,4,64,256]{3,2,1,0:T(8,128)(2,1)S(1)}, bf16[4,4,64,256]{3,2,1,0:T(8,128)(2,1)S(1)}, u32[]{:S(2)}, u32[]{:S(2)}) collective-permute-start(bf16[4,4,64,256]{3,2,1,0:T(8,128)(2,1)S(1)} %bitcast.48), channel_id=1, source_target_pairs={{0,8},{1,17},{2,10},{3,19},{4,12},{5,21},{6,14},{7,23},{8,0},{9,25... | collective-permute-start | bytes 1572872 | tf_op jit(solution)/shard_map/cond/branch_1_fun/ppermute | solution.py:307
  100.3 25.0 %collective-permute-start.27 = (bf16[4,4,64,256]{3,2,1,0:T(8,128)(2,1)S(1)}, bf16[4,4,64,256]{3,2,1,0:T(8,128)(2,1)S(1)}, u32[]{:S(2)}, u32[]{:S(2)}) collective-permute-start(bf16[4,4,64,256]{3,2,1,0:T(8,128)(2,1)S(1)} %bitcast.43), channel_id=1, source_target_pairs={{0,8},{1,17},{2,10},{3,19},{4,12},{5,21},{6,14},{7,23},{8,0},{9,25... | collective-permute-start | bytes 1572872 | tf_op jit(solution)/shard_map/cond/branch_1_fun/ppermute | solution.py:307
  108.2 29.6 %collective-permute-start.25 = (bf16[2,4,64,256]{3,2,1,0:T(8,128)(2,1)S(1)}, bf16[2,4,64,256]{3,2,1,0:T(8,128)(2,1)S(1)}, u32[]{:S(2)}, u32[]{:S(2)}) collective-permute-start(bf16[2,4,64,256]{3,2,1,0:T(8,128)(2,1)S(1)} %bitcast.58), channel_id=1, source_target_pairs={{0,8},{1,17},{2,10},{3,19},{4,12},{5,21},{6,14},{7,23},{8,0},{9,25... | collective-permute-start | bytes 786440 | tf_op jit(solution)/shard_map/cond/branch_1_fun/ppermute | solution.py:307
  108.9 27.6 %collective-permute-start.26 = (bf16[2,4,64,256]{3,2,1,0:T(8,128)(2,1)S(1)}, bf16[2,4,64,256]{3,2,1,0:T(8,128)(2,1)S(1)}, u32[]{:S(2)}, u32[]{:S(2)}) collective-permute-start(bf16[2,4,64,256]{3,2,1,0:T(8,128)(2,1)S(1)} %bitcast.61), channel_id=1, source_target_pairs={{0,8},{1,17},{2,10},{3,19},{4,12},{5,21},{6,14},{7,23},{8,0},{9,25... | collective-permute-start | bytes 786440 | tf_op jit(solution)/shard_map/cond/branch_1_fun/ppermute | solution.py:307
  119.1 22.9 %collective-permute-start.24 = (bf16[4,4,64,128]{3,2,1,0:T(8,128)(2,1)S(1)}, bf16[4,4,64,128]{3,2,1,0:T(8,128)(2,1)S(1)}, u32[]{:S(2)}, u32[]{:S(2)}) collective-permute-start(bf16[4,4,64,128]{3,2,1,0:T(8,128)(2,1)S(1)} %bitcast.62), channel_id=1, source_target_pairs={{0,8},{1,17},{2,10},{3,19},{4,12},{5,21},{6,14},{7,23},{8,0},{9,25... | collective-permute-start | bytes 786440 | tf_op jit(solution)/shard_map/cond/branch_1_fun/ppermute | solution.py:307
  119.8 27.6 %collective-permute-start.23 = (bf16[4,4,64,128]{3,2,1,0:T(8,128)(2,1)S(1)}, bf16[4,4,64,128]{3,2,1,0:T(8,128)(2,1)S(1)}, u32[]{:S(2)}, u32[]{:S(2)}) collective-permute-start(bf16[4,4,64,128]{3,2,1,0:T(8,128)(2,1)S(1)} %bitcast.60), channel_id=1, source_target_pairs={{0,8},{1,17},{2,10},{3,19},{4,12},{5,21},{6,14},{7,23},{8,0},{9,25... | collective-permute-start | bytes 786440 | tf_op jit(solution)/shard_map/cond/branch_1_fun/ppermute | solution.py:307
  (12 other events, 77.2 us)
where the time goes:
time: 151 us; the launch traced here: 150 us
  Pallas kernels  46 us (30%)
  waiting for transfers between devices  35.1 us (23%)
  local copies, waits for them, and re-layouts  28.7 us (19%)
  starting transfers between devices  26.5 us (18%)
  blocking collectives  8.6 us (6%)
  between operations  2.17 us (1%)
  other arithmetic  1.55 us (1%)
    pallas_call x7, Pallas kernels, blocks_call(): pl.pallas_call(functools.partial(block_kernel, hi, rows, narrow, first),...  30.8 us
    ppermute x12, waiting for transfers between devices, route(): return lax.ppermute(x, ('chan', 'sec'), pairs)  21.2 us
    ppermute x12, starting transfers between devices, route(): return lax.ppermute(x, ('chan', 'sec'), pairs)  18.8 us
    gather x6, local copies, waits for them, and re-layouts, packs(): jnp.take(x, asked[(gap - 1) * slots:gap * slots], axis=0, mode='clip')  11.8 us
    ppermute x6, waiting for transfers between devices, over_chips(): lax.ppermute(x, 'sec', [(s, s ^ 2 * gap) for s in range(n_sec)])  11.6 us
    pallas_call x7, Pallas kernels, add_call(): pl.pallas_call(functools.partial(add_kernel, len(terms), span), in_specs=...  9.5 us
    psum x1, blocking collectives, on_device(): lax.psum(jnp.where(mine, jnp.concatenate([wants, n_wide])[None], 0), 'sec')  8.6 us
    ppermute x6, starting transfers between devices, over_chips(): lax.ppermute(x, 'sec', [(s, s ^ 2 * gap) for s in range(n_sec)])  7.11 us
  transfers between devices with their start and end apart: 20, of which 9 were waited for; matrix products, arithmetic and copies ran while one was open for 19% of the time, Pallas kernels for 29%

commit v1 on v0

--- a/solution.py
+++ b/solution.py
@@ -159,15 +159,38 @@
     )(me, dims, table)
 
 
+def pack_kernel(hi, slots, asked, *refs):
+    sources, outs = refs[:hi], refs[hi:]
+    rows = sources[0].shape[1]
+    for gap, out in enumerate(outs):
+        for n in range(slots):
+            for i in range(hi):
+                out[n, i * rows : (i + 1) * rows] = sources[i][asked[gap * slots + n]]
+
+
+def pack_call(slots, gaps, asked, sources):
+    hi = len(sources)
+    _, rows, width = sources[0].shape
+    vmem = pl.BlockSpec(memory_space=pltpu.VMEM)
+    return pl.pallas_call(
+        functools.partial(pack_kernel, hi, slots),
+        in_specs=[SMEM] + [vmem] * hi,
+        out_specs=[vmem] * gaps,
+        out_shape=[jax.ShapeDtypeStruct((slots, hi * rows, width), sources[0].dtype)] * gaps,
+        compiler_params=pltpu.CompilerParams(vmem_limit_bytes=24 * 2**20),
+        cost_estimate=pl.CostEstimate(
+            flops=0, bytes_accessed=4 * hi * sources[0].size, transcendentals=0
+        ),
+    )(asked, *sources)
+
+
 def block_kernel(hi, rows, narrow, first, order, right_dims, near, row, mpo, psi, *refs):
-    lefts, rights = refs[: 2 * hi], refs[2 * hi : 3 * hi]
-    keep, send = refs[3 * hi :]
+    nears, far, rights = refs[:hi], refs[hi], refs[hi + 1 : 2 * hi + 1]
+    keep, send = refs[2 * hi + 1 :]
     states = psi.shape[1]
     k = order[pl.program_id(0) + first]
-    is_near = jnp.full(lefts[0].shape[1:], near[k], jnp.int32) > 0
-    stacked = jnp.concatenate(
-        [jnp.where(is_near, lefts[2 * i][0], lefts[2 * i + 1][0]) for i in range(hi)], axis=0
-    )
+    is_near = jnp.full(far.shape[1:], near[k], jnp.int32) > 0
+    stacked = jnp.where(is_near, jnp.concatenate([left[0] for left in nears], axis=0), far[0])
     parts = [
         jnp.dot(stacked, psi[0, p], preferred_element_type=jnp.float32) for p in range(states)
     ]
@@ -222,7 +245,8 @@
         in_specs=[
             pl.BlockSpec((1, states, width, across), lambda *at: by_block(*at) + (0,)),
         ]
-        + [pl.BlockSpec((1, rows, width), by_row(far)) for _ in range(hi) for far in range(2)]
+        + [pl.BlockSpec((1, rows, width), by_row(0))] * hi
+        + [pl.BlockSpec((1, hi * rows, width), by_row(1))]
         + [pl.BlockSpec((1, across, across), by_block)]
         + [pl.BlockSpec((1, across, across), lambda k, *_: (k + first - base, 0, 0))] * (hi - 1),
         out_specs=[
@@ -246,30 +270,36 @@
     )(*scalars, mpo, psi, *lefts, right, *others)
 
 
-def add_kernel(terms, span, order, *refs):
+def add_kernel(group, order, *refs):
     out, total, sems = refs[-3:]
-    across = refs[0].shape[-1]
-    copies = []
-    for k in range(span.stop - span.start):
-        acc = refs[0][k].astype(jnp.float32)
-        for j in range(1, terms):
-            acc = acc + refs[j][k].astype(jnp.float32)
-        total[k, :, :, :across] = acc.astype(total.dtype)
-        if across < total.shape[-1]:
-            total[k, :, :, across:] = jnp.zeros(acc.shape[:-1] + (total.shape[-1] - across,), total.dtype)
-        copy = pltpu.make_async_copy(total.at[k], out.at[order[k + span.start]], sems.at[k])
-        copy.start()
-        copies.append(copy)
+    copies, at = [], 0
+    for span, terms in group:
+        refs, parts = refs[terms:], refs[:terms]
+        across = parts[0].shape[-1]
+        for k in range(span.stop - span.start):
+            acc = parts[0][k].astype(jnp.float32)
+            for part in parts[1:]:
+                acc = acc + part[k].astype(jnp.float32)
+            total[at, :, :, :across] = acc.astype(total.dtype)
+            if across < total.shape[-1]:
+                blank = acc.shape[:-1] + (total.shape[-1] - across,)
+                total[at, :, :, across:] = jnp.zeros(blank, total.dtype)
+            copy = pltpu.make_async_copy(total.at[at], out.at[order[k + span.start]], sems.at[at])
+            copy.start()
+            copies.append(copy)
+            at += 1
     for copy in copies:
         copy.wait()
 
 
-def add_call(shape, span, order, terms, out):
-    count = span.stop - span.start
+def add_call(shape, order, group, out):
+    count = sum(span.stop - span.start for span, _ in group)
+    flat = [x for _, terms in group for x in terms]
+    size = sum(x.size for x in flat)
     return pl.pallas_call(
-        functools.partial(add_kernel, len(terms), span),
+        functools.partial(add_kernel, [(span, len(terms)) for span, terms in group]),
         in_specs=[SMEM]
-        + [pl.BlockSpec(memory_space=pltpu.VMEM)] * len(terms)
+        + [pl.BlockSpec(memory_space=pltpu.VMEM)] * len(flat)
         + ([] if out is None else [ANY]),
         out_specs=ANY,
         out_shape=jax.ShapeDtypeStruct(shape, jnp.bfloat16),
@@ -277,12 +307,10 @@
             pltpu.VMEM((count,) + shape[1:], jnp.bfloat16),
             pltpu.SemaphoreType.DMA((count,)),
         ],
-        input_output_aliases={} if out is None else {1 + len(terms): 0},
+        input_output_aliases={} if out is None else {1 + len(flat): 0},
         compiler_params=pltpu.CompilerParams(vmem_limit_bytes=24 * 2**20),
-        cost_estimate=pl.CostEstimate(
-            flops=terms[0].size, bytes_accessed=6 * terms[0].size, transcendentals=0
-        ),
-    )(order, *terms, *([] if out is None else [out]))
+        cost_estimate=pl.CostEstimate(flops=size, bytes_accessed=3 * size, transcendentals=0),
+    )(order, *flat, *([] if out is None else [out]))
 
 
 def on_device(n_chan, n_sec, psi, mpo, left_env, right_env, left_dims, right_dims, dest_owner, left_slot):
@@ -311,12 +339,6 @@
 
     def beside(x):
         return lax.ppermute(x, "sec", [(s, s ^ 1) for s in range(n_sec)])
-
-    def packs(x, asked):
-        return [
-            jnp.take(x, asked[(gap - 1) * slots : gap * slots], axis=0, mode="clip")
-            for gap in range(1, n_sec // 2)
-        ]
 
     def over_chips(packed):
         parts = []
@@ -347,7 +369,7 @@
         order = scalars[0]
         moved = [to_partners(first)]
         sources = [shards[0]] + swapped
-        packed = [packs(x, asked) for x in sources]
+        packed = pack_call(slots, n_sec // 2 - 1, asked, sources)
         bounds = [(0, caps[0])]
         if cap > caps[0]:
             bounds.append((caps[0], cap))
@@ -366,9 +388,7 @@
             thin = jnp.take(right, order[cap:], axis=0, mode="clip")[:, :half, :half]
             moved.append(to_partners(after(thin, packed)))
         total = len(spans)
-        lefts = []
-        for x, parts in zip(sources, packed):
-            lefts += [x, over_chips(parts)]
+        lefts = sources + [over_chips(packed)]
         shape = (blocks, states, own_rows, width)
         out, terms = None, []
         for span, narrow, base, n in spans:
@@ -378,8 +398,10 @@
             mpo_all = after(mpo_all, keep, *([] if terms else moved[1:]))
             terms.append([keep] + [route(send[j - 1], 0, j) for j in range(1, lo)])
         terms[0][0] = after(terms[0][0], terms[-1][0])
-        for m in range(total):
-            out = add_call(shape, spans[m][0], order, terms[m], out)
+        pairs = [(span[0], term) for span, term in zip(spans, terms)]
+        alone = max(total - 3, 0)
+        for group in [[pair] for pair in pairs[:alone]] + [pairs[alone:]]:
+            out = add_call(shape, order, group, out)
         return out
 
     which = sum((most_wide > cap).astype(jnp.int32) for cap in caps[:-1])

time: 151 us -> 172 us (1.14)
  waiting for transfers between devices: 35.1 us -> 70.8 us
  local copies, waits for them, and re-layouts: 28.7 us -> 17.3 us
  starting transfers between devices: 26.5 us -> 22 us
    ppermute x12, waiting for transfers between devices: 21.2 us -> 47 us  [route(): return lax.ppermute(x, ('chan', 'sec'), pairs)]
    gather x6 -> x0, local copies, waits for them, and re-layouts: 11.8 us -> none  [packs(): jnp.take(x, asked[(gap - 1) * slots:gap * slots], axis=0, mode='clip')]
    ppermute x6 -> x3, waiting for transfers between devices: 11.6 us -> 21.4 us  [over_chips(): lax.ppermute(x, 'sec', [(s, s ^ 2 * gap) for s in range(n_sec)])]
    ppermute x6 -> x3, starting transfers between devices: 7.11 us -> 3.49 us  [over_chips(): lax.ppermute(x, 'sec', [(s, s ^ 2 * gap) for s in range(n_sec)])]
    pallas_call x7 -> x6, Pallas kernels: 9.5 us -> 10.1 us  [the longest x5 7.16 us: add_call(): pl.pallas_call(functools.partial(add_kernel, [(span, len(terms)) for span...]
  transfers between devices with their start and end apart: 20 -> 17, of which waited for: 9 -> 10; matrix products, arithmetic and copies ran while one was open for 19% -> 11% of each run, Pallas kernels for 29% -> 25%
where the time goes in v1:
time: 172 us; the launch traced here: 171 us
  waiting for transfers between devices  70.8 us (41%)
  Pallas kernels  46.5 us (27%)
  starting transfers between devices  22 us (13%)
  local copies, waits for them, and re-layouts  17.3 us (10%)
  blocking collectives  8.6 us (5%)
  other arithmetic  2.86 us (2%)
  between operations  2.31 us (1%)
    ppermute x12, waiting for transfers between devices, route(): return lax.ppermute(x, ('chan', 'sec'), pairs)  47 us
    pallas_call x7, Pallas kernels, blocks_call(): pl.pallas_call(functools.partial(block_kernel, hi, rows, narrow, first),...  29.6 us
    ppermute x3, waiting for transfers between devices, over_chips(): lax.ppermute(x, 'sec', [(s, s ^ 2 * gap) for s in range(n_sec)])  21.4 us
    ppermute x12, starting transfers between devices, route(): return lax.ppermute(x, ('chan', 'sec'), pairs)  18 us
    psum x1, blocking collectives, on_device(): lax.psum(jnp.where(mine, jnp.concatenate([wants, n_wide])[None], 0), 'sec')  8.6 us
    pallas_call x5, Pallas kernels, add_call(): pl.pallas_call(functools.partial(add_kernel, [(span, len(terms)) for span...  7.16 us
    pallas_call x1, Pallas kernels, plan_call(): pl.pallas_call(functools.partial(plan_kernel, half, sectors, slots), in_s...  4.13 us
    gather x1, local copies, waits for them, and re-layouts, on_device(): jnp.take(right, order[:caps[0]], axis=0, mode='clip')  3.79 us
  transfers between devices with their start and end apart: 17, of which 10 were waited for; matrix products, arithmetic and copies ran while one was open for 11% of the time, Pallas kernels for 25%

profile of v1, /device:TPU:0, one launch (start us, length us, event | category | flops | bytes accessed | tf_op | source)
XLA Modules:
  0.0 171.4 jit_solution(15115815813674685787)
XLA Ops:
  4.8 2.7 %shard_map.87 = (bf16[16,128,256]{2,1,0:T(8,128)(2,1)}, bf16[16,128,256]{2,1,0:T(8,128)(2,1)S(1)}) custom-call(s32[2]{0:T(128)S(1)} %pad_add_fusion.1.where, s32[8]{0:T(128)S(1)} %copy-done.1, s32[8]{0:T(128)S(1)} %collective-permute-done.49.side_dims, bf16[8,256,256]{2,1,0:T(8,128)(2,1)S(1)} %bitcast.39, ...), custom_call_target="tpu_custom_call" | custom-call | flops 1048576 | bytes 4194304 | tf_op jit(solution)/shard_map/pallas_call | solution.py:65
  7.5 4.0 %collective-permute-start.51 = (bf16[16,128,256]{2,1,0:T(8,128)(2,1)S(1)}, bf16[16,128,256]{2,1,0:T(8,128)(2,1)}, u32[]{:S(2)}, u32[]{:S(2)}) collective-permute-start(bf16[16,128,256]{2,1,0:T(8,128)(2,1)S(1)} %get-tuple-element.253), channel_id=1, source_target_pairs={{0,16},{1,9},{2,18},{3,11},{4,20},{5,13},{6,22},{7,15},{8,24},{9,1... | collective-permute-start | bytes 3145736 | tf_op jit(solution)/shard_map/ppermute | solution.py:335
  14.2 8.6 %psum.7.table = s32[8,25]{1,0:T(8,128)} all-reduce(s32[8,25]{1,0:T(8,128)S(1)} %broadcast_select_fusion), channel_id=1, replica_groups=mesh['chan'=4,'sec'=8] {'sec'}, use_global_device_ids=true, to_apply=%region_1.2 | all-reduce | flops 200 | bytes 1600 | tf_op jit(solution)/shard_map/psum | solution.py:354
  22.8 4.1 %shard_map.86 = (s32[24]{0:T(128)S(1)}, s32[24]{0:T(128)S(1)}, s32[24]{0:T(128)S(1)}, s32[18]{0:T(128)S(1)}, s32[1]{0:T(128)}) custom-call(s32[1]{0:T(128)} %bitcast.27.me, s32[24]{0:T(128)} %dims.1, s32[8,25]{1,0:T(8,128)} %psum.7.table), custom_call_target="tpu_custom_call" | custom-call | bytes 800 | tf_op jit(solution)/shard_map/pallas_call | solution.py:152
  30.9 3.8 %gather_fusion.6 = bf16[14,256,256]{2,1,0:T(8,128)(2,1)} fusion(bf16[24,256,256]{2,1,0:T(8,128)(2,1)} %bitcast.77, s32[1024]{0:T(1024)S(1)} %pad_clamp_fusion.6), kind=kCustom, calls=%fused_computation.6 | custom fusion | bytes 3670072 | tf_op jit(solution)/shard_map/jit(_take)/gather | solution.py:366
  34.8 136.4 %conditional.1 = (bf16[24,4,64,256]{3,2,1,0:T(8,128)(2,1)}) conditional(s32[]{:T(128)} %bitcast.30, (s32[18]{0:T(128)S(1)}, bf16[16,128,256]{2,1,0:T(8,128)(2,1)}, bf16[16,128,256]{2,1,0:T(8,128)(2,1)}, bf16[14,256,256]{2,1,0:T(8,128)(2,1)}, s32[24]{0:T(128)S(1)}, /*index=5*/s32[24]{0:T(128)S(1)}, s32[24]{0:T(128)S(1)}, ...), branch_computations={%region_2.3_spmd, %region_3.4_spmd, %region_4.5_spmd, %region_5.6_... | conditional | flops 6445597696 | bytes 174859136 | solution.py:408
  37.2 2.9 %branch_1_fun.13 = (bf16[6,256,256]{2,1,0:T(8,128)(2,1)}, bf16[6,256,256]{2,1,0:T(8,128)(2,1)}, bf16[6,256,256]{2,1,0:T(8,128)(2,1)S(1)}) custom-call(s32[18]{0:T(128)S(1)} %get-tuple-element.139.asked, bf16[16,128,256]{2,1,0:T(8,128)(2,1)} %get-tuple-element.137.refs_0_, bf16[16,128,256]{2,1,0:T(8,128)(2,1)} %get-tuple-element.138.refs_1_), custom_call_target="tpu_custom_call" | custom-call | bytes 4194304 | tf_op jit(solution)/shard_map/cond/branch_1_fun/pallas_call | solution.py:175
  43.7 2.5 %gather_fusion.1 = bf16[2,256,256]{2,1,0:T(8,128)(2,1)S(1)} fusion(bf16[24,256,256]{2,1,0:T(8,128)(2,1)} %get-tuple-element.143.refs_3_, s32[1024]{0:T(1024)S(1)} %get-tuple-element.261), kind=kCustom, calls=%fused_computation.1 | custom fusion | bytes 524296 | tf_op jit(solution)/shard_map/cond/branch_1_fun/jit(_take)/gather | solution.py:376
  47.0 3.5 %gather_fusion.2 = bf16[8,256,256]{2,1,0:T(8,128)(2,1)} fusion(bf16[24,256,256]{2,1,0:T(8,128)(2,1)} %get-tuple-element.143.refs_3_, s32[1024]{0:T(1024)S(1)} %get-tuple-element.260), kind=kCustom, calls=%fused_computation.2 | custom fusion | bytes 2097184 | tf_op jit(solution)/shard_map/cond/branch_1_fun/jit(_take)/gather | solution.py:388
  51.5 9.4 %collective-permute-done.11 = bf16[6,256,256]{2,1,0:T(8,128)(2,1)} collective-permute-done((bf16[6,256,256]{2,1,0:T(8,128)(2,1)}, bf16[6,256,256]{2,1,0:T(8,128)(2,1)}, u32[]{:S(2)}, u32[]{:S(2)}) %collective-permute-start.11) | collective-permute-done | bytes 786464 | tf_op jit(solution)/shard_map/cond/branch_1_fun/ppermute | solution.py:346
  62.8 12.0 %collective-permute-done.12 = bf16[6,256,256]{2,1,0:T(8,128)(2,1)} collective-permute-done((bf16[6,256,256]{2,1,0:T(8,128)(2,1)}, bf16[6,256,256]{2,1,0:T(8,128)(2,1)}, u32[]{:S(2)}, u32[]{:S(2)}) %collective-permute-start.12) | collective-permute-done | bytes 786464 | tf_op jit(solution)/shard_map/cond/branch_1_fun/ppermute | solution.py:346
  78.0 5.4 %branch_1_fun.14 = (bf16[4,4,64,256]{3,2,1,0:T(8,128)(2,1)S(1)}, bf16[1,4,4,64,256]{4,3,2,1,0:T(8,128)(2,1)S(1)}) custom-call(s32[24]{0:T(128)S(1)} %get-tuple-element.131.order, s32[24]{0:T(128)S(1)} %get-tuple-element.132.right_dims, s32[24]{0:T(128)S(1)} %get-tuple-element.133.near, s32[24]{0:T(128)S(1)} %get-tuple-element.134.row, ...), custom_call_target="tpu_custom_call" | custom-call | flops 1073741824 | bytes 5242880 | tf_op jit(solution)/shard_map/cond/branch_1_fun/pallas_call | solution.py:257
  83.3 30.0 %collective-permute-done.16.refs_4_ = bf16[8,128,128]{2,1,0:T(8,128)(2,1)S(1)} collective-permute-done((bf16[8,128,128]{2,1,0:T(8,128)(2,1)S(1)}, bf16[8,128,128]{2,1,0:T(8,128)(2,1)S(1)}, u32[]{:S(2)}, u32[]{:S(2)}) %collective-permute-start.16) | collective-permute-done | bytes 262176 | tf_op jit(solution)/shard_map/cond/branch_1_fun/ppermute | solution.py:335
  113.3 4.6 %collective-permute-start.23 = (bf16[4,4,64,256]{3,2,1,0:T(8,128)(2,1)S(1)}, bf16[4,4,64,256]{3,2,1,0:T(8,128)(2,1)S(1)}, u32[]{:S(2)}, u32[]{:S(2)}) collective-permute-start(bf16[4,4,64,256]{3,2,1,0:T(8,128)(2,1)S(1)} %bitcast.45), channel_id=1, source_target_pairs={{0,8},{1,17},{2,10},{3,19},{4,12},{5,21},{6,14},{7,23},{8,0},{9,25... | collective-permute-start | bytes 1572872 | tf_op jit(solution)/shard_map/cond/branch_1_fun/ppermute | solution.py:335
  118.0 4.7 %branch_1_fun.15 = (bf16[4,4,64,256]{3,2,1,0:T(8,128)(2,1)S(1)}, bf16[1,4,4,64,256]{4,3,2,1,0:T(8,128)(2,1)S(1)}) custom-call(s32[24]{0:T(128)S(1)} %get-tuple-element.131.order, s32[24]{0:T(128)S(1)} %get-tuple-element.132.right_dims, s32[24]{0:T(128)S(1)} %get-tuple-element.133.near, s32[24]{0:T(128)S(1)} %get-tuple-element.134.row, ...), custom_call_target="tpu_custom_call" | custom-call | flops 1073741824 | bytes 5242880 | tf_op jit(solution)/shard_map/cond/branch_1_fun/pallas_call | solution.py:257
  122.7 4.7 %branch_1_fun.16 = (bf16[4,4,64,256]{3,2,1,0:T(8,128)(2,1)S(1)}, bf16[1,4,4,64,256]{4,3,2,1,0:T(8,128)(2,1)S(1)}) custom-call(s32[24]{0:T(128)S(1)} %get-tuple-element.131.order, s32[24]{0:T(128)S(1)} %get-tuple-element.132.right_dims, s32[24]{0:T(128)S(1)} %get-tuple-element.133.near, s32[24]{0:T(128)S(1)} %get-tuple-element.134.row, ...), custom_call_target="tpu_custom_call" | custom-call | flops 1073741824 | bytes 5242880 | tf_op jit(solution)/shard_map/cond/branch_1_fun/pallas_call | solution.py:257
  129.5 3.0 %branch_1_fun.17 = (bf16[2,4,64,256]{3,2,1,0:T(8,128)(2,1)S(1)}, bf16[1,2,4,64,256]{4,3,2,1,0:T(8,128)(2,1)S(1)}) custom-call(s32[24]{0:T(128)S(1)} %get-tuple-element.131.order, s32[24]{0:T(128)S(1)} %get-tuple-element.132.right_dims, s32[24]{0:T(128)S(1)} %get-tuple-element.133.near, s32[24]{0:T(128)S(1)} %get-tuple-element.134.row, ...), custom_call_target="tpu_custom_call" | custom-call | flops 536870912 | bytes 2621440 | tf_op jit(solution)/shard_map/cond/branch_1_fun/pallas_call | solution.py:257
  132.5 3.0 %branch_1_fun.18 = (bf16[2,4,64,256]{3,2,1,0:T(8,128)(2,1)S(1)}, bf16[1,2,4,64,256]{4,3,2,1,0:T(8,128)(2,1)S(1)}) custom-call(s32[24]{0:T(128)S(1)} %get-tuple-element.131.order, s32[24]{0:T(128)S(1)} %get-tuple-element.132.right_dims, s32[24]{0:T(128)S(1)} %get-tuple-element.133.near, s32[24]{0:T(128)S(1)} %get-tuple-element.134.row, ...), custom_call_target="tpu_custom_call" | custom-call | flops 536870912 | bytes 2621440 | tf_op jit(solution)/shard_map/cond/branch_1_fun/pallas_call | solution.py:257
  137.6 4.5 %branch_1_fun.19 = (bf16[4,4,64,128]{3,2,1,0:T(8,128)(2,1)S(1)}, bf16[1,4,4,64,128]{4,3,2,1,0:T(8,128)(2,1)S(1)}) custom-call(s32[24]{0:T(128)S(1)} %get-tuple-element.131.order, s32[24]{0:T(128)S(1)} %get-tuple-element.132.right_dims, s32[24]{0:T(128)S(1)} %get-tuple-element.133.near, s32[24]{0:T(128)S(1)} %get-tuple-element.134.row, ...), custom_call_target="tpu_custom_call" | custom-call | flops 402653184 | bytes 2621440 | tf_op jit(solution)/shard_map/cond/branch_1_fun/pallas_call | solution.py:257
  142.1 4.4 %branch_1_fun.20 = (bf16[4,4,64,128]{3,2,1,0:T(8,128)(2,1)S(1)}, bf16[1,4,4,64,128]{4,3,2,1,0:T(8,128)(2,1)S(1)}) custom-call(s32[24]{0:T(128)S(1)} %get-tuple-element.131.order, s32[24]{0:T(128)S(1)} %get-tuple-element.132.right_dims, s32[24]{0:T(128)S(1)} %get-tuple-element.133.near, s32[24]{0:T(128)S(1)} %get-tuple-element.134.row, ...), custom_call_target="tpu_custom_call" | custom-call | flops 402653184 | bytes 2621440 | tf_op jit(solution)/shard_map/cond/branch_1_fun/pallas_call | solution.py:257
  147.0 5.1 %collective-permute-done.22.refs_1_ = bf16[4,4,64,256]{3,2,1,0:T(8,128)(2,1)S(1)} collective-permute-done((bf16[4,4,64,256]{3,2,1,0:T(8,128)(2,1)S(1)}, bf16[4,4,64,256]{3,2,1,0:T(8,128)(2,1)S(1)}, u32[]{:S(2)}, u32[]{:S(2)}) %collective-permute-start.22) | collective-permute-done | bytes 524320 | tf_op jit(solution)/shard_map/cond/branch_1_fun/ppermute | solution.py:335
  154.9 2.8 %collective-permute-done.21.refs_1_ = bf16[4,4,64,256]{3,2,1,0:T(8,128)(2,1)S(1)} collective-permute-done((bf16[4,4,64,256]{3,2,1,0:T(8,128)(2,1)S(1)}, bf16[4,4,64,256]{3,2,1,0:T(8,128)(2,1)S(1)}, u32[]{:S(2)}, u32[]{:S(2)}) %collective-permute-start.21) | collective-permute-done | bytes 524320 | tf_op jit(solution)/shard_map/cond/branch_1_fun/ppermute | solution.py:335
  159.1 4.2 %collective-permute-done.20.refs_1_ = bf16[2,4,64,256]{3,2,1,0:T(8,128)(2,1)S(1)} collective-permute-done((bf16[2,4,64,256]{3,2,1,0:T(8,128)(2,1)S(1)}, bf16[2,4,64,256]{3,2,1,0:T(8,128)(2,1)S(1)}, u32[]{:S(2)}, u32[]{:S(2)}) %collective-permute-start.20) | collective-permute-done | bytes 262176 | tf_op jit(solution)/shard_map/cond/branch_1_fun/ppermute | solution.py:335
  166.1 2.8 %collective-permute-done.18.refs_3_ = bf16[4,4,64,128]{3,2,1,0:T(8,128)(2,1)S(1)} collective-permute-done((bf16[4,4,64,128]{3,2,1,0:T(8,128)(2,1)S(1)}, bf16[4,4,64,128]{3,2,1,0:T(8,128)(2,1)S(1)}, u32[]{:S(2)}, u32[]{:S(2)}) %collective-permute-start.18) | collective-permute-done | bytes 262176 | tf_op jit(solution)/shard_map/cond/branch_1_fun/ppermute | solution.py:335
  (66 shorter events, 35.6 us)
Async XLA Ops:
  0.0 3.0 %collective-permute-start.50 = (bf16[8,256,256]{2,1,0:T(8,128)(2,1)}, bf16[8,256,256]{2,1,0:T(8,128)(2,1)S(1)}, u32[]{:S(2)}, u32[]{:S(2)}) collective-permute-start(bf16[8,256,256]{2,1,0:T(8,128)(2,1)} %bitcast.38), channel_id=1, source_target_pairs={{0,1},{1,0},{2,3},{3,2},{4,5},{5,4},{6,7},{7,6},{8,9},{9,8},{10,11... | collective-permute-start | bytes 3145736 | tf_op jit(solution)/shard_map/ppermute | solution.py:341
  0.5 2.5 %collective-permute-start.49 = (s32[8]{0:T(128)}, s32[8]{0:T(128)S(1)}, u32[]{:S(2)}, u32[]{:S(2)}) collective-permute-start(s32[8]{0:T(128)} %own_dims.1), channel_id=1, source_target_pairs={{0,1},{1,0},{2,3},{3,2},{4,5},{5,4},{6,7},{7,6},{8,9},{9,8},{10,11... | collective-permute-start | bytes 104 | tf_op jit(solution)/shard_map/ppermute | solution.py:341
  7.5 27.2 %copy-start.15 = (s32[24]{0:T(128)S(1)}, s32[24]{0:T(128)}, u32[]{:S(2)}) copy-start(s32[24]{0:T(128)} %dims.1) | copy-start | bytes 292
  7.5 27.2 %collective-permute-start.51 = (bf16[16,128,256]{2,1,0:T(8,128)(2,1)S(1)}, bf16[16,128,256]{2,1,0:T(8,128)(2,1)}, u32[]{:S(2)}, u32[]{:S(2)}) collective-permute-start(bf16[16,128,256]{2,1,0:T(8,128)(2,1)S(1)} %get-tuple-element.253), channel_id=1, source_target_pairs={{0,16},{1,9},{2,18},{3,11},{4,20},{5,13},{6,22},{7,15},{8,24},{9,1... | collective-permute-start | bytes 3145736 | tf_op jit(solution)/shard_map/ppermute | solution.py:335
  27.0 7.7 %collective-permute-start.52 = (f32[4,4]{1,0:T(4,128)}, f32[4,4]{1,0:T(4,128)S(1)}, u32[]{:S(2)}, u32[]{:S(2)}) collective-permute-start(f32[4,4]{1,0:T(4,128)} %bitcast.83), channel_id=1, source_target_pairs={{0,16},{1,9},{2,18},{3,11},{4,20},{5,13},{6,22},{7,15},{8,24},{9,1... | collective-permute-start | bytes 200 | tf_op jit(solution)/shard_map/ppermute | solution.py:335
  35.0 43.0 %collective-permute-start.14 = (bf16[14,256,256]{2,1,0:T(8,128)(2,1)}, bf16[14,256,256]{2,1,0:T(8,128)(2,1)S(1)}, u32[]{:S(2)}, u32[]{:S(2)}) collective-permute-start(bf16[14,256,256]{2,1,0:T(8,128)(2,1)} %get-tuple-element.144), channel_id=1, source_target_pairs={{0,16},{1,9},{2,18},{3,11},{4,20},{5,13},{6,22},{7,15},{8,24},{9,1... | collective-permute-start | bytes 5505032 | tf_op jit(solution)/shard_map/cond/branch_1_fun/ppermute | solution.py:335
  40.1 20.8 %collective-permute-start.11 = (bf16[6,256,256]{2,1,0:T(8,128)(2,1)}, bf16[6,256,256]{2,1,0:T(8,128)(2,1)}, u32[]{:S(2)}, u32[]{:S(2)}) collective-permute-start(bf16[6,256,256]{2,1,0:T(8,128)(2,1)} %get-tuple-element.140), channel_id=1, source_target_pairs={{0,2},{1,3},{2,0},{3,1},{4,6},{5,7},{6,4},{7,5},{8,10},{9,11},{10,... | collective-permute-start | bytes 2359304 | tf_op jit(solution)/shard_map/cond/branch_1_fun/ppermute | solution.py:346
  41.6 33.3 %collective-permute-start.12 = (bf16[6,256,256]{2,1,0:T(8,128)(2,1)}, bf16[6,256,256]{2,1,0:T(8,128)(2,1)}, u32[]{:S(2)}, u32[]{:S(2)}) collective-permute-start(bf16[6,256,256]{2,1,0:T(8,128)(2,1)} %get-tuple-element.141), channel_id=1, source_target_pairs={{0,4},{1,5},{2,6},{3,7},{4,0},{5,1},{6,2},{7,3},{8,12},{9,13},{10,... | collective-permute-start | bytes 2359304 | tf_op jit(solution)/shard_map/cond/branch_1_fun/ppermute | solution.py:346
  43.1 33.0 %collective-permute-start.13 = (bf16[6,256,256]{2,1,0:T(8,128)(2,1)S(1)}, bf16[6,256,256]{2,1,0:T(8,128)(2,1)}, u32[]{:S(2)}, u32[]{:S(2)}) collective-permute-start(bf16[6,256,256]{2,1,0:T(8,128)(2,1)S(1)} %get-tuple-element.142), channel_id=1, source_target_pairs={{0,6},{1,7},{2,4},{3,5},{4,2},{5,3},{6,0},{7,1},{8,14},{9,15},{10,... | collective-permute-start | bytes 2359304 | tf_op jit(solution)/shard_map/cond/branch_1_fun/ppermute | solution.py:346
  46.2 37.2 %collective-permute-start.15 = (bf16[2,256,256]{2,1,0:T(8,128)(2,1)S(1)}, bf16[2,256,256]{2,1,0:T(8,128)(2,1)S(1)}, u32[]{:S(2)}, u32[]{:S(2)}) collective-permute-start(bf16[2,256,256]{2,1,0:T(8,128)(2,1)S(1)} %gather_fusion.1), channel_id=1, source_target_pairs={{0,16},{1,9},{2,18},{3,11},{4,20},{5,13},{6,22},{7,15},{8,24},{9,1... | collective-permute-start | bytes 786440 | tf_op jit(solution)/shard_map/cond/branch_1_fun/ppermute | solution.py:335
  51.5 26.5 %copy-start.9 = (bf16[16,128,256]{2,1,0:T(8,128)(2,1)S(1)}, bf16[16,128,256]{2,1,0:T(8,128)(2,1)}, u32[]{:S(2)}) copy-start(bf16[16,128,256]{2,1,0:T(8,128)(2,1)} %get-tuple-element.137.refs_0_) | copy-start | bytes 3145732 | tf_op jit(solution)/shard_map/cond
  60.9 52.5 %collective-permute-start.16 = (bf16[8,128,128]{2,1,0:T(8,128)(2,1)S(1)}, bf16[8,128,128]{2,1,0:T(8,128)(2,1)S(1)}, u32[]{:S(2)}, u32[]{:S(2)}) collective-permute-start(bf16[8,128,128]{2,1,0:T(8,128)(2,1)S(1)} %slice.46), channel_id=1, source_target_pairs={{0,16},{1,9},{2,18},{3,11},{4,20},{5,13},{6,22},{7,15},{8,24},{9,1... | collective-permute-start | bytes 786440 | tf_op jit(solution)/shard_map/cond/branch_1_fun/ppermute | solution.py:335
  76.0 41.9 %slice-start.3 = ((s8[12582912]{0:T(1024)(128)(4,1)}), s8[4194304]{0:T(1024)(128)(4,1)S(1)}, s32[]{:S(2)}) async-start(s8[12582912]{0:T(1024)(128)(4,1)} %bitcast.69), calls=%async_computation.3 | async-start | bytes 8388608 | tf_op jit(solution)/shard_map/cond
  78.0 40.0 %slice-start.4 = ((s8[12582912]{0:T(1024)(128)(4,1)}), s8[4194304]{0:T(1024)(128)(4,1)S(1)}, s32[]{:S(2)}) async-start(s8[12582912]{0:T(1024)(128)(4,1)} %bitcast.69), calls=%async_computation.4 | async-start | bytes 8388608 | tf_op jit(solution)/shard_map/cond
  78.0 40.0 %slice-start.5 = ((s8[12582912]{0:T(1024)(128)(4,1)}), s8[4194304]{0:T(1024)(128)(4,1)S(1)}, s32[]{:S(2)}) async-start(s8[12582912]{0:T(1024)(128)(4,1)} %bitcast.69), calls=%async_computation.5 | async-start | bytes 8388608 | tf_op jit(solution)/shard_map/cond
  113.3 33.2 %collective-permute-start.23 = (bf16[4,4,64,256]{3,2,1,0:T(8,128)(2,1)S(1)}, bf16[4,4,64,256]{3,2,1,0:T(8,128)(2,1)S(1)}, u32[]{:S(2)}, u32[]{:S(2)}) collective-permute-start(bf16[4,4,64,256]{3,2,1,0:T(8,128)(2,1)S(1)} %bitcast.45), channel_id=1, source_target_pairs={{0,8},{1,17},{2,10},{3,19},{4,12},{5,21},{6,14},{7,23},{8,0},{9,25... | collective-permute-start | bytes 1572872 | tf_op jit(solution)/shard_map/cond/branch_1_fun/ppermute | solution.py:335
  122.6 29.5 %collective-permute-start.22 = (bf16[4,4,64,256]{3,2,1,0:T(8,128)(2,1)S(1)}, bf16[4,4,64,256]{3,2,1,0:T(8,128)(2,1)S(1)}, u32[]{:S(2)}, u32[]{:S(2)}) collective-permute-start(bf16[4,4,64,256]{3,2,1,0:T(8,128)(2,1)S(1)} %bitcast.51), channel_id=1, source_target_pairs={{0,8},{1,17},{2,10},{3,19},{4,12},{5,21},{6,14},{7,23},{8,0},{9,25... | collective-permute-start | bytes 1572872 | tf_op jit(solution)/shard_map/cond/branch_1_fun/ppermute | solution.py:335
  122.7 6.8 %copy-start.10 = (bf16[16,128,256]{2,1,0:T(8,128)(2,1)S(1)}, bf16[16,128,256]{2,1,0:T(8,128)(2,1)}, u32[]{:S(2)}) copy-start(bf16[16,128,256]{2,1,0:T(8,128)(2,1)} %get-tuple-element.137.refs_0_) | copy-start | bytes 3145732 | tf_op jit(solution)/shard_map/cond
  127.4 30.3 %collective-permute-start.21 = (bf16[4,4,64,256]{3,2,1,0:T(8,128)(2,1)S(1)}, bf16[4,4,64,256]{3,2,1,0:T(8,128)(2,1)S(1)}, u32[]{:S(2)}, u32[]{:S(2)}) collective-permute-start(bf16[4,4,64,256]{3,2,1,0:T(8,128)(2,1)S(1)} %bitcast.43), channel_id=1, source_target_pairs={{0,8},{1,17},{2,10},{3,19},{4,12},{5,21},{6,14},{7,23},{8,0},{9,25... | collective-permute-start | bytes 1572872 | tf_op jit(solution)/shard_map/cond/branch_1_fun/ppermute | solution.py:335
  135.5 29.1 %collective-permute-start.17 = (bf16[2,4,64,256]{3,2,1,0:T(8,128)(2,1)S(1)}, bf16[2,4,64,256]{3,2,1,0:T(8,128)(2,1)S(1)}, u32[]{:S(2)}, u32[]{:S(2)}) collective-permute-start(bf16[2,4,64,256]{3,2,1,0:T(8,128)(2,1)S(1)} %bitcast.58), channel_id=1, source_target_pairs={{0,8},{1,17},{2,10},{3,19},{4,12},{5,21},{6,14},{7,23},{8,0},{9,25... | collective-permute-start | bytes 786440 | tf_op jit(solution)/shard_map/cond/branch_1_fun/ppermute | solution.py:335
  135.6 6.5 %copy-start.4 = (bf16[24,256,256]{2,1,0:T(8,128)(2,1)S(1)}, bf16[24,256,256]{2,1,0:T(8,128)(2,1)}, u32[]{:S(2)}) copy-start(bf16[24,256,256]{2,1,0:T(8,128)(2,1)} %get-tuple-element.143.refs_3_) | copy-start | bytes 9437188 | tf_op jit(solution)/shard_map/cond
  135.6 27.7 %collective-permute-start.20 = (bf16[2,4,64,256]{3,2,1,0:T(8,128)(2,1)S(1)}, bf16[2,4,64,256]{3,2,1,0:T(8,128)(2,1)S(1)}, u32[]{:S(2)}, u32[]{:S(2)}) collective-permute-start(bf16[2,4,64,256]{3,2,1,0:T(8,128)(2,1)S(1)} %bitcast.60), channel_id=1, source_target_pairs={{0,8},{1,17},{2,10},{3,19},{4,12},{5,21},{6,14},{7,23},{8,0},{9,25... | collective-permute-start | bytes 786440 | tf_op jit(solution)/shard_map/cond/branch_1_fun/ppermute | solution.py:335
  146.6 19.6 %collective-permute-start.19 = (bf16[4,4,64,128]{3,2,1,0:T(8,128)(2,1)S(1)}, bf16[4,4,64,128]{3,2,1,0:T(8,128)(2,1)S(1)}, u32[]{:S(2)}, u32[]{:S(2)}) collective-permute-start(bf16[4,4,64,128]{3,2,1,0:T(8,128)(2,1)S(1)} %bitcast.63), channel_id=1, source_target_pairs={{0,8},{1,17},{2,10},{3,19},{4,12},{5,21},{6,14},{7,23},{8,0},{9,25... | collective-permute-start | bytes 786440 | tf_op jit(solution)/shard_map/cond/branch_1_fun/ppermute | solution.py:335
  152.1 16.9 %collective-permute-start.18 = (bf16[4,4,64,128]{3,2,1,0:T(8,128)(2,1)S(1)}, bf16[4,4,64,128]{3,2,1,0:T(8,128)(2,1)S(1)}, u32[]{:S(2)}, u32[]{:S(2)}) collective-permute-start(bf16[4,4,64,128]{3,2,1,0:T(8,128)(2,1)S(1)} %bitcast.61), channel_id=1, source_target_pairs={{0,8},{1,17},{2,10},{3,19},{4,12},{5,21},{6,14},{7,23},{8,0},{9,25... | collective-permute-start | bytes 786440 | tf_op jit(solution)/shard_map/cond/branch_1_fun/ppermute | solution.py:335
  (2 other events, 1.9 us)

commit v2 on v1

--- a/solution.py
+++ b/solution.py
@@ -362,7 +362,7 @@
     mpo_own = after(mpo[0], order)
     mpo_all = jnp.stack([mpo_own] + to_partners(mpo_own)).reshape(hi, states * states)
     scalars = (order, right_dims, near, row)
-    caps = sorted({max(2, blocks * q // 12) for q in (7, 8, 9)} | {blocks})
+    caps = sorted({max(2, blocks * q // 12) for q in (7, 8, 9, 10)} | {blocks})
     first = after(jnp.take(right, order[: caps[0]], axis=0, mode="clip"), swapped)
 
     def run(cap, scalars, asked, shards, swapped, first, mpo_all):
@@ -395,6 +395,8 @@
             keep, send = blocks_call(
                 hi, lo, own_rows, narrow, span, base, scalars, mpo_all, psi, lefts, right, moved[n]
             )
+            if not terms:
+                send = after(send, *moved[1:])
             mpo_all = after(mpo_all, keep, *([] if terms else moved[1:]))
             terms.append([keep] + [route(send[j - 1], 0, j) for j in range(1, lo)])
         terms[0][0] = after(terms[0][0], terms[-1][0])

time: 172 us -> 172 us (level)
  no operation moved by 1% of the time
where the time goes in v2:
time: 172 us
  waiting for transfers between devices  71.4 us (42%)
  Pallas kernels  46.5 us (27%)
  starting transfers between devices  21.5 us (12%)
  local copies, waits for them, and re-layouts  17.3 us (10%)
  blocking collectives  8.6 us (5%)
  other arithmetic  2.86 us (2%)
  between operations  2.57 us (1%)
    ppermute x12, waiting for transfers between devices, route(): return lax.ppermute(x, ('chan', 'sec'), pairs)  48.1 us
    pallas_call x7, Pallas kernels, blocks_call(): pl.pallas_call(functools.partial(block_kernel, hi, rows, narrow, first),...  29.7 us
    ppermute x3, waiting for transfers between devices, over_chips(): lax.ppermute(x, 'sec', [(s, s ^ 2 * gap) for s in range(n_sec)])  21 us
    ppermute x12, starting transfers between devices, route(): return lax.ppermute(x, ('chan', 'sec'), pairs)  17.5 us
    psum x1, blocking collectives, on_device(): lax.psum(jnp.where(mine, jnp.concatenate([wants, n_wide])[None], 0), 'sec')  8.6 us
    pallas_call x5, Pallas kernels, add_call(): pl.pallas_call(functools.partial(add_kernel, [(span, len(terms)) for span...  7.16 us
    pallas_call x1, Pallas kernels, plan_call(): pl.pallas_call(functools.partial(plan_kernel, half, sectors, slots), in_s...  4.13 us
    gather x1, local copies, waits for them, and re-layouts, on_device(): jnp.take(right, order[:caps[0]], axis=0, mode='clip')  3.81 us
  transfers between devices with their start and end apart: 17, of which 10 were waited for; matrix products, arithmetic and copies ran while one was open for 11% of the time, Pallas kernels for 25%

profile of v2, /device:TPU:0, one launch (start us, length us, event | category | flops | bytes accessed | tf_op | source)
XLA Modules:
  0.0 171.7 jit_solution(7679934015644061281)
XLA Ops:
  4.8 2.7 %shard_map.88 = (bf16[16,128,256]{2,1,0:T(8,128)(2,1)}, bf16[16,128,256]{2,1,0:T(8,128)(2,1)S(1)}) custom-call(s32[2]{0:T(128)S(1)} %pad_add_fusion.1.where, s32[8]{0:T(128)S(1)} %copy-done.1, s32[8]{0:T(128)S(1)} %collective-permute-done.62.side_dims, bf16[8,256,256]{2,1,0:T(8,128)(2,1)S(1)} %bitcast.46, ...), custom_call_target="tpu_custom_call" | custom-call | flops 1048576 | bytes 4194304 | tf_op jit(solution)/shard_map/pallas_call | solution.py:65
  7.6 4.0 %collective-permute-start.64 = (bf16[16,128,256]{2,1,0:T(8,128)(2,1)S(1)}, bf16[16,128,256]{2,1,0:T(8,128)(2,1)}, u32[]{:S(2)}, u32[]{:S(2)}) collective-permute-start(bf16[16,128,256]{2,1,0:T(8,128)(2,1)S(1)} %get-tuple-element.318), channel_id=1, source_target_pairs={{0,16},{1,9},{2,18},{3,11},{4,20},{5,13},{6,22},{7,15},{8,24},{9,1... | collective-permute-start | bytes 3145736 | tf_op jit(solution)/shard_map/ppermute | solution.py:335
  14.3 8.6 %psum.7.table = s32[8,25]{1,0:T(8,128)} all-reduce(s32[8,25]{1,0:T(8,128)S(1)} %broadcast_select_fusion), channel_id=1, replica_groups=mesh['chan'=4,'sec'=8] {'sec'}, use_global_device_ids=true, to_apply=%region_1.2 | all-reduce | flops 200 | bytes 1600 | tf_op jit(solution)/shard_map/psum | solution.py:354
  22.9 4.1 %shard_map.87 = (s32[24]{0:T(128)S(1)}, s32[24]{0:T(128)S(1)}, s32[24]{0:T(128)S(1)}, s32[18]{0:T(128)S(1)}, s32[1]{0:T(128)}) custom-call(s32[1]{0:T(128)} %bitcast.34.me, s32[24]{0:T(128)} %dims.1, s32[8,25]{1,0:T(8,128)} %psum.7.table), custom_call_target="tpu_custom_call" | custom-call | bytes 800 | tf_op jit(solution)/shard_map/pallas_call | solution.py:152
  31.1 3.8 %gather_fusion.8 = bf16[14,256,256]{2,1,0:T(8,128)(2,1)} fusion(bf16[24,256,256]{2,1,0:T(8,128)(2,1)} %bitcast.95, s32[1024]{0:T(1024)S(1)} %pad_clamp_fusion.8), kind=kCustom, calls=%fused_computation.8 | custom fusion | bytes 3670072 | tf_op jit(solution)/shard_map/jit(_take)/gather | solution.py:366
  35.1 136.4 %conditional.1 = (bf16[24,4,64,256]{3,2,1,0:T(8,128)(2,1)}) conditional(s32[]{:T(128)} %bitcast.37, (s32[18]{0:T(128)S(1)}, bf16[16,128,256]{2,1,0:T(8,128)(2,1)}, bf16[16,128,256]{2,1,0:T(8,128)(2,1)}, bf16[14,256,256]{2,1,0:T(8,128)(2,1)}, s32[24]{0:T(128)S(1)}, /*index=5*/s32[24]{0:T(128)S(1)}, s32[24]{0:T(128)S(1)}, ...), branch_computations={%region_2.3_spmd, %region_3.4_spmd, %region_4.5_spmd, %region_5.6_... | conditional | flops 6445597696 | bytes 174859136 | solution.py:410
  37.3 2.9 %branch_1_fun.13 = (bf16[6,256,256]{2,1,0:T(8,128)(2,1)}, bf16[6,256,256]{2,1,0:T(8,128)(2,1)}, bf16[6,256,256]{2,1,0:T(8,128)(2,1)S(1)}) custom-call(s32[18]{0:T(128)S(1)} %get-tuple-element.163.asked, bf16[16,128,256]{2,1,0:T(8,128)(2,1)} %get-tuple-element.161.refs_0_, bf16[16,128,256]{2,1,0:T(8,128)(2,1)} %get-tuple-element.162.refs_1_), custom_call_target="tpu_custom_call" | custom-call | bytes 4194304 | tf_op jit(solution)/shard_map/cond/branch_1_fun/pallas_call | solution.py:175
  43.8 2.5 %gather_fusion.1 = bf16[2,256,256]{2,1,0:T(8,128)(2,1)S(1)} fusion(bf16[24,256,256]{2,1,0:T(8,128)(2,1)} %get-tuple-element.167.refs_3_, s32[1024]{0:T(1024)S(1)} %get-tuple-element.326), kind=kCustom, calls=%fused_computation.1 | custom fusion | bytes 524296 | tf_op jit(solution)/shard_map/cond/branch_1_fun/jit(_take)/gather | solution.py:376
  47.3 3.5 %gather_fusion.2 = bf16[8,256,256]{2,1,0:T(8,128)(2,1)} fusion(bf16[24,256,256]{2,1,0:T(8,128)(2,1)} %get-tuple-element.167.refs_3_, s32[1024]{0:T(1024)S(1)} %get-tuple-element.325), kind=kCustom, calls=%fused_computation.2 | custom fusion | bytes 2097184 | tf_op jit(solution)/shard_map/cond/branch_1_fun/jit(_take)/gather | solution.py:388
  51.7 9.2 %collective-permute-done.11 = bf16[6,256,256]{2,1,0:T(8,128)(2,1)} collective-permute-done((bf16[6,256,256]{2,1,0:T(8,128)(2,1)}, bf16[6,256,256]{2,1,0:T(8,128)(2,1)}, u32[]{:S(2)}, u32[]{:S(2)}) %collective-permute-start.11) | collective-permute-done | bytes 786464 | tf_op jit(solution)/shard_map/cond/branch_1_fun/ppermute | solution.py:346
  63.1 11.7 %collective-permute-done.12 = bf16[6,256,256]{2,1,0:T(8,128)(2,1)} collective-permute-done((bf16[6,256,256]{2,1,0:T(8,128)(2,1)}, bf16[6,256,256]{2,1,0:T(8,128)(2,1)}, u32[]{:S(2)}, u32[]{:S(2)}) %collective-permute-start.12) | collective-permute-done | bytes 786464 | tf_op jit(solution)/shard_map/cond/branch_1_fun/ppermute | solution.py:346
  78.1 5.4 %branch_1_fun.14 = (bf16[4,4,64,256]{3,2,1,0:T(8,128)(2,1)S(1)}, bf16[1,4,4,64,256]{4,3,2,1,0:T(8,128)(2,1)S(1)}) custom-call(s32[24]{0:T(128)S(1)} %get-tuple-element.155.order, s32[24]{0:T(128)S(1)} %get-tuple-element.156.right_dims, s32[24]{0:T(128)S(1)} %get-tuple-element.157.near, s32[24]{0:T(128)S(1)} %get-tuple-element.158.row, ...), custom_call_target="tpu_custom_call" | custom-call | flops 1073741824 | bytes 5242880 | tf_op jit(solution)/shard_map/cond/branch_1_fun/pallas_call | solution.py:257
  83.5 30.4 %collective-permute-done.16.refs_4_ = bf16[8,128,128]{2,1,0:T(8,128)(2,1)S(1)} collective-permute-done((bf16[8,128,128]{2,1,0:T(8,128)(2,1)S(1)}, bf16[8,128,128]{2,1,0:T(8,128)(2,1)S(1)}, u32[]{:S(2)}, u32[]{:S(2)}) %collective-permute-start.16) | collective-permute-done | bytes 262176 | tf_op jit(solution)/shard_map/cond/branch_1_fun/ppermute | solution.py:335
  113.9 3.9 %collective-permute-start.23 = (bf16[4,4,64,256]{3,2,1,0:T(8,128)(2,1)S(1)}, bf16[4,4,64,256]{3,2,1,0:T(8,128)(2,1)S(1)}, u32[]{:S(2)}, u32[]{:S(2)}) collective-permute-start(bf16[4,4,64,256]{3,2,1,0:T(8,128)(2,1)S(1)} %bitcast.54), channel_id=1, source_target_pairs={{0,8},{1,17},{2,10},{3,19},{4,12},{5,21},{6,14},{7,23},{8,0},{9,25... | collective-permute-start | bytes 1572872 | tf_op jit(solution)/shard_map/cond/branch_1_fun/ppermute | solution.py:335
  117.8 4.7 %branch_1_fun.15 = (bf16[4,4,64,256]{3,2,1,0:T(8,128)(2,1)S(1)}, bf16[1,4,4,64,256]{4,3,2,1,0:T(8,128)(2,1)S(1)}) custom-call(s32[24]{0:T(128)S(1)} %get-tuple-element.155.order, s32[24]{0:T(128)S(1)} %get-tuple-element.156.right_dims, s32[24]{0:T(128)S(1)} %get-tuple-element.157.near, s32[24]{0:T(128)S(1)} %get-tuple-element.158.row, ...), custom_call_target="tpu_custom_call" | custom-call | flops 1073741824 | bytes 5242880 | tf_op jit(solution)/shard_map/cond/branch_1_fun/pallas_call | solution.py:257
  122.6 4.7 %branch_1_fun.16 = (bf16[4,4,64,256]{3,2,1,0:T(8,128)(2,1)S(1)}, bf16[1,4,4,64,256]{4,3,2,1,0:T(8,128)(2,1)S(1)}) custom-call(s32[24]{0:T(128)S(1)} %get-tuple-element.155.order, s32[24]{0:T(128)S(1)} %get-tuple-element.156.right_dims, s32[24]{0:T(128)S(1)} %get-tuple-element.157.near, s32[24]{0:T(128)S(1)} %get-tuple-element.158.row, ...), custom_call_target="tpu_custom_call" | custom-call | flops 1073741824 | bytes 5242880 | tf_op jit(solution)/shard_map/cond/branch_1_fun/pallas_call | solution.py:257
  129.3 3.0 %branch_1_fun.17 = (bf16[2,4,64,256]{3,2,1,0:T(8,128)(2,1)S(1)}, bf16[1,2,4,64,256]{4,3,2,1,0:T(8,128)(2,1)S(1)}) custom-call(s32[24]{0:T(128)S(1)} %get-tuple-element.155.order, s32[24]{0:T(128)S(1)} %get-tuple-element.156.right_dims, s32[24]{0:T(128)S(1)} %get-tuple-element.157.near, s32[24]{0:T(128)S(1)} %get-tuple-element.158.row, ...), custom_call_target="tpu_custom_call" | custom-call | flops 536870912 | bytes 2621440 | tf_op jit(solution)/shard_map/cond/branch_1_fun/pallas_call | solution.py:257
  132.4 3.0 %branch_1_fun.18 = (bf16[2,4,64,256]{3,2,1,0:T(8,128)(2,1)S(1)}, bf16[1,2,4,64,256]{4,3,2,1,0:T(8,128)(2,1)S(1)}) custom-call(s32[24]{0:T(128)S(1)} %get-tuple-element.155.order, s32[24]{0:T(128)S(1)} %get-tuple-element.156.right_dims, s32[24]{0:T(128)S(1)} %get-tuple-element.157.near, s32[24]{0:T(128)S(1)} %get-tuple-element.158.row, ...), custom_call_target="tpu_custom_call" | custom-call | flops 536870912 | bytes 2621440 | tf_op jit(solution)/shard_map/cond/branch_1_fun/pallas_call | solution.py:257
  137.5 4.5 %branch_1_fun.19 = (bf16[4,4,64,128]{3,2,1,0:T(8,128)(2,1)S(1)}, bf16[1,4,4,64,128]{4,3,2,1,0:T(8,128)(2,1)S(1)}) custom-call(s32[24]{0:T(128)S(1)} %get-tuple-element.155.order, s32[24]{0:T(128)S(1)} %get-tuple-element.156.right_dims, s32[24]{0:T(128)S(1)} %get-tuple-element.157.near, s32[24]{0:T(128)S(1)} %get-tuple-element.158.row, ...), custom_call_target="tpu_custom_call" | custom-call | flops 402653184 | bytes 2621440 | tf_op jit(solution)/shard_map/cond/branch_1_fun/pallas_call | solution.py:257
  142.0 4.4 %branch_1_fun.20 = (bf16[4,4,64,128]{3,2,1,0:T(8,128)(2,1)S(1)}, bf16[1,4,4,64,128]{4,3,2,1,0:T(8,128)(2,1)S(1)}) custom-call(s32[24]{0:T(128)S(1)} %get-tuple-element.155.order, s32[24]{0:T(128)S(1)} %get-tuple-element.156.right_dims, s32[24]{0:T(128)S(1)} %get-tuple-element.157.near, s32[24]{0:T(128)S(1)} %get-tuple-element.158.row, ...), custom_call_target="tpu_custom_call" | custom-call | flops 402653184 | bytes 2621440 | tf_op jit(solution)/shard_map/cond/branch_1_fun/pallas_call | solution.py:257
  146.8 5.6 %collective-permute-done.22.refs_1_ = bf16[4,4,64,256]{3,2,1,0:T(8,128)(2,1)S(1)} collective-permute-done((bf16[4,4,64,256]{3,2,1,0:T(8,128)(2,1)S(1)}, bf16[4,4,64,256]{3,2,1,0:T(8,128)(2,1)S(1)}, u32[]{:S(2)}, u32[]{:S(2)}) %collective-permute-start.22) | collective-permute-done | bytes 524320 | tf_op jit(solution)/shard_map/cond/branch_1_fun/ppermute | solution.py:335
  155.2 2.8 %collective-permute-done.21.refs_1_ = bf16[4,4,64,256]{3,2,1,0:T(8,128)(2,1)S(1)} collective-permute-done((bf16[4,4,64,256]{3,2,1,0:T(8,128)(2,1)S(1)}, bf16[4,4,64,256]{3,2,1,0:T(8,128)(2,1)S(1)}, u32[]{:S(2)}, u32[]{:S(2)}) %collective-permute-start.21) | collective-permute-done | bytes 524320 | tf_op jit(solution)/shard_map/cond/branch_1_fun/ppermute | solution.py:335
  159.4 4.2 %collective-permute-done.20.refs_1_ = bf16[2,4,64,256]{3,2,1,0:T(8,128)(2,1)S(1)} collective-permute-done((bf16[2,4,64,256]{3,2,1,0:T(8,128)(2,1)S(1)}, bf16[2,4,64,256]{3,2,1,0:T(8,128)(2,1)S(1)}, u32[]{:S(2)}, u32[]{:S(2)}) %collective-permute-start.20) | collective-permute-done | bytes 262176 | tf_op jit(solution)/shard_map/cond/branch_1_fun/ppermute | solution.py:335
  166.4 2.8 %collective-permute-done.18.refs_3_ = bf16[4,4,64,128]{3,2,1,0:T(8,128)(2,1)S(1)} collective-permute-done((bf16[4,4,64,128]{3,2,1,0:T(8,128)(2,1)S(1)}, bf16[4,4,64,128]{3,2,1,0:T(8,128)(2,1)S(1)}, u32[]{:S(2)}, u32[]{:S(2)}) %collective-permute-start.18) | collective-permute-done | bytes 262176 | tf_op jit(solution)/shard_map/cond/branch_1_fun/ppermute | solution.py:335
  (66 shorter events, 35.9 us)
Async XLA Ops:
  0.0 3.0 %collective-permute-start.63 = (bf16[8,256,256]{2,1,0:T(8,128)(2,1)}, bf16[8,256,256]{2,1,0:T(8,128)(2,1)S(1)}, u32[]{:S(2)}, u32[]{:S(2)}) collective-permute-start(bf16[8,256,256]{2,1,0:T(8,128)(2,1)} %bitcast.45), channel_id=1, source_target_pairs={{0,1},{1,0},{2,3},{3,2},{4,5},{5,4},{6,7},{7,6},{8,9},{9,8},{10,11... | collective-permute-start | bytes 3145736 | tf_op jit(solution)/shard_map/ppermute | solution.py:341
  0.5 2.5 %collective-permute-start.62 = (s32[8]{0:T(128)}, s32[8]{0:T(128)S(1)}, u32[]{:S(2)}, u32[]{:S(2)}) collective-permute-start(s32[8]{0:T(128)} %own_dims.1), channel_id=1, source_target_pairs={{0,1},{1,0},{2,3},{3,2},{4,5},{5,4},{6,7},{7,6},{8,9},{9,8},{10,11... | collective-permute-start | bytes 104 | tf_op jit(solution)/shard_map/ppermute | solution.py:341
  7.6 27.5 %copy-start.16 = (s32[24]{0:T(128)S(1)}, s32[24]{0:T(128)}, u32[]{:S(2)}) copy-start(s32[24]{0:T(128)} %dims.1) | copy-start | bytes 292
  7.6 27.5 %collective-permute-start.64 = (bf16[16,128,256]{2,1,0:T(8,128)(2,1)S(1)}, bf16[16,128,256]{2,1,0:T(8,128)(2,1)}, u32[]{:S(2)}, u32[]{:S(2)}) collective-permute-start(bf16[16,128,256]{2,1,0:T(8,128)(2,1)S(1)} %get-tuple-element.318), channel_id=1, source_target_pairs={{0,16},{1,9},{2,18},{3,11},{4,20},{5,13},{6,22},{7,15},{8,24},{9,1... | collective-permute-start | bytes 3145736 | tf_op jit(solution)/shard_map/ppermute | solution.py:335
  27.0 7.9 %collective-permute-start.65 = (f32[4,4]{1,0:T(4,128)}, f32[4,4]{1,0:T(4,128)S(1)}, u32[]{:S(2)}, u32[]{:S(2)}) collective-permute-start(f32[4,4]{1,0:T(4,128)} %bitcast.102), channel_id=1, source_target_pairs={{0,16},{1,9},{2,18},{3,11},{4,20},{5,13},{6,22},{7,15},{8,24},{9,1... | collective-permute-start | bytes 200 | tf_op jit(solution)/shard_map/ppermute | solution.py:335
  35.3 42.8 %collective-permute-start.14 = (bf16[14,256,256]{2,1,0:T(8,128)(2,1)}, bf16[14,256,256]{2,1,0:T(8,128)(2,1)S(1)}, u32[]{:S(2)}, u32[]{:S(2)}) collective-permute-start(bf16[14,256,256]{2,1,0:T(8,128)(2,1)} %get-tuple-element.168), channel_id=1, source_target_pairs={{0,16},{1,9},{2,18},{3,11},{4,20},{5,13},{6,22},{7,15},{8,24},{9,1... | collective-permute-start | bytes 5505032 | tf_op jit(solution)/shard_map/cond/branch_1_fun/ppermute | solution.py:335
  40.2 20.8 %collective-permute-start.11 = (bf16[6,256,256]{2,1,0:T(8,128)(2,1)}, bf16[6,256,256]{2,1,0:T(8,128)(2,1)}, u32[]{:S(2)}, u32[]{:S(2)}) collective-permute-start(bf16[6,256,256]{2,1,0:T(8,128)(2,1)} %get-tuple-element.164), channel_id=1, source_target_pairs={{0,2},{1,3},{2,0},{3,1},{4,6},{5,7},{6,4},{7,5},{8,10},{9,11},{10,... | collective-permute-start | bytes 2359304 | tf_op jit(solution)/shard_map/cond/branch_1_fun/ppermute | solution.py:346
  41.6 33.3 %collective-permute-start.12 = (bf16[6,256,256]{2,1,0:T(8,128)(2,1)}, bf16[6,256,256]{2,1,0:T(8,128)(2,1)}, u32[]{:S(2)}, u32[]{:S(2)}) collective-permute-start(bf16[6,256,256]{2,1,0:T(8,128)(2,1)} %get-tuple-element.165), channel_id=1, source_target_pairs={{0,4},{1,5},{2,6},{3,7},{4,0},{5,1},{6,2},{7,3},{8,12},{9,13},{10,... | collective-permute-start | bytes 2359304 | tf_op jit(solution)/shard_map/cond/branch_1_fun/ppermute | solution.py:346
  43.1 33.0 %collective-permute-start.13 = (bf16[6,256,256]{2,1,0:T(8,128)(2,1)S(1)}, bf16[6,256,256]{2,1,0:T(8,128)(2,1)}, u32[]{:S(2)}, u32[]{:S(2)}) collective-permute-start(bf16[6,256,256]{2,1,0:T(8,128)(2,1)S(1)} %get-tuple-element.166), channel_id=1, source_target_pairs={{0,6},{1,7},{2,4},{3,5},{4,2},{5,3},{6,0},{7,1},{8,14},{9,15},{10,... | collective-permute-start | bytes 2359304 | tf_op jit(solution)/shard_map/cond/branch_1_fun/ppermute | solution.py:346
  46.3 37.2 %collective-permute-start.15 = (bf16[2,256,256]{2,1,0:T(8,128)(2,1)S(1)}, bf16[2,256,256]{2,1,0:T(8,128)(2,1)S(1)}, u32[]{:S(2)}, u32[]{:S(2)}) collective-permute-start(bf16[2,256,256]{2,1,0:T(8,128)(2,1)S(1)} %gather_fusion.1), channel_id=1, source_target_pairs={{0,16},{1,9},{2,18},{3,11},{4,20},{5,13},{6,22},{7,15},{8,24},{9,1... | collective-permute-start | bytes 786440 | tf_op jit(solution)/shard_map/cond/branch_1_fun/ppermute | solution.py:335
  51.7 26.4 %copy-start.9 = (bf16[16,128,256]{2,1,0:T(8,128)(2,1)S(1)}, bf16[16,128,256]{2,1,0:T(8,128)(2,1)}, u32[]{:S(2)}) copy-start(bf16[16,128,256]{2,1,0:T(8,128)(2,1)} %get-tuple-element.161.refs_0_) | copy-start | bytes 3145732 | tf_op jit(solution)/shard_map/cond
  61.0 53.0 %collective-permute-start.16 = (bf16[8,128,128]{2,1,0:T(8,128)(2,1)S(1)}, bf16[8,128,128]{2,1,0:T(8,128)(2,1)S(1)}, u32[]{:S(2)}, u32[]{:S(2)}) collective-permute-start(bf16[8,128,128]{2,1,0:T(8,128)(2,1)S(1)} %slice.59), channel_id=1, source_target_pairs={{0,16},{1,9},{2,18},{3,11},{4,20},{5,13},{6,22},{7,15},{8,24},{9,1... | collective-permute-start | bytes 786440 | tf_op jit(solution)/shard_map/cond/branch_1_fun/ppermute | solution.py:335
  76.0 41.8 %slice-start.3 = ((s8[12582912]{0:T(1024)(128)(4,1)}), s8[4194304]{0:T(1024)(128)(4,1)S(1)}, s32[]{:S(2)}) async-start(s8[12582912]{0:T(1024)(128)(4,1)} %bitcast.83), calls=%async_computation.3 | async-start | bytes 8388608 | tf_op jit(solution)/shard_map/cond
  78.1 39.7 %slice-start.4 = ((s8[12582912]{0:T(1024)(128)(4,1)}), s8[4194304]{0:T(1024)(128)(4,1)S(1)}, s32[]{:S(2)}) async-start(s8[12582912]{0:T(1024)(128)(4,1)} %bitcast.83), calls=%async_computation.4 | async-start | bytes 8388608 | tf_op jit(solution)/shard_map/cond
  78.1 39.7 %slice-start.5 = ((s8[12582912]{0:T(1024)(128)(4,1)}), s8[4194304]{0:T(1024)(128)(4,1)S(1)}, s32[]{:S(2)}) async-start(s8[12582912]{0:T(1024)(128)(4,1)} %bitcast.83), calls=%async_computation.5 | async-start | bytes 8388608 | tf_op jit(solution)/shard_map/cond
  113.9 32.5 %collective-permute-start.23 = (bf16[4,4,64,256]{3,2,1,0:T(8,128)(2,1)S(1)}, bf16[4,4,64,256]{3,2,1,0:T(8,128)(2,1)S(1)}, u32[]{:S(2)}, u32[]{:S(2)}) collective-permute-start(bf16[4,4,64,256]{3,2,1,0:T(8,128)(2,1)S(1)} %bitcast.54), channel_id=1, source_target_pairs={{0,8},{1,17},{2,10},{3,19},{4,12},{5,21},{6,14},{7,23},{8,0},{9,25... | collective-permute-start | bytes 1572872 | tf_op jit(solution)/shard_map/cond/branch_1_fun/ppermute | solution.py:335
  122.5 29.9 %collective-permute-start.22 = (bf16[4,4,64,256]{3,2,1,0:T(8,128)(2,1)S(1)}, bf16[4,4,64,256]{3,2,1,0:T(8,128)(2,1)S(1)}, u32[]{:S(2)}, u32[]{:S(2)}) collective-permute-start(bf16[4,4,64,256]{3,2,1,0:T(8,128)(2,1)S(1)} %bitcast.61), channel_id=1, source_target_pairs={{0,8},{1,17},{2,10},{3,19},{4,12},{5,21},{6,14},{7,23},{8,0},{9,25... | collective-permute-start | bytes 1572872 | tf_op jit(solution)/shard_map/cond/branch_1_fun/ppermute | solution.py:335
  122.6 6.8 %copy-start.10 = (bf16[16,128,256]{2,1,0:T(8,128)(2,1)S(1)}, bf16[16,128,256]{2,1,0:T(8,128)(2,1)}, u32[]{:S(2)}) copy-start(bf16[16,128,256]{2,1,0:T(8,128)(2,1)} %get-tuple-element.161.refs_0_) | copy-start | bytes 3145732 | tf_op jit(solution)/shard_map/cond
  127.3 30.7 %collective-permute-start.21 = (bf16[4,4,64,256]{3,2,1,0:T(8,128)(2,1)S(1)}, bf16[4,4,64,256]{3,2,1,0:T(8,128)(2,1)S(1)}, u32[]{:S(2)}, u32[]{:S(2)}) collective-permute-start(bf16[4,4,64,256]{3,2,1,0:T(8,128)(2,1)S(1)} %bitcast.51), channel_id=1, source_target_pairs={{0,8},{1,17},{2,10},{3,19},{4,12},{5,21},{6,14},{7,23},{8,0},{9,25... | collective-permute-start | bytes 1572872 | tf_op jit(solution)/shard_map/cond/branch_1_fun/ppermute | solution.py:335
  135.4 29.5 %collective-permute-start.17 = (bf16[2,4,64,256]{3,2,1,0:T(8,128)(2,1)S(1)}, bf16[2,4,64,256]{3,2,1,0:T(8,128)(2,1)S(1)}, u32[]{:S(2)}, u32[]{:S(2)}) collective-permute-start(bf16[2,4,64,256]{3,2,1,0:T(8,128)(2,1)S(1)} %bitcast.70), channel_id=1, source_target_pairs={{0,8},{1,17},{2,10},{3,19},{4,12},{5,21},{6,14},{7,23},{8,0},{9,25... | collective-permute-start | bytes 786440 | tf_op jit(solution)/shard_map/cond/branch_1_fun/ppermute | solution.py:335
  135.5 6.5 %copy-start.4 = (bf16[24,256,256]{2,1,0:T(8,128)(2,1)S(1)}, bf16[24,256,256]{2,1,0:T(8,128)(2,1)}, u32[]{:S(2)}) copy-start(bf16[24,256,256]{2,1,0:T(8,128)(2,1)} %get-tuple-element.167.refs_3_) | copy-start | bytes 9437188 | tf_op jit(solution)/shard_map/cond
  135.5 28.2 %collective-permute-start.20 = (bf16[2,4,64,256]{3,2,1,0:T(8,128)(2,1)S(1)}, bf16[2,4,64,256]{3,2,1,0:T(8,128)(2,1)S(1)}, u32[]{:S(2)}, u32[]{:S(2)}) collective-permute-start(bf16[2,4,64,256]{3,2,1,0:T(8,128)(2,1)S(1)} %bitcast.72), channel_id=1, source_target_pairs={{0,8},{1,17},{2,10},{3,19},{4,12},{5,21},{6,14},{7,23},{8,0},{9,25... | collective-permute-start | bytes 786440 | tf_op jit(solution)/shard_map/cond/branch_1_fun/ppermute | solution.py:335
  146.4 20.0 %collective-permute-start.19 = (bf16[4,4,64,128]{3,2,1,0:T(8,128)(2,1)S(1)}, bf16[4,4,64,128]{3,2,1,0:T(8,128)(2,1)S(1)}, u32[]{:S(2)}, u32[]{:S(2)}) collective-permute-start(bf16[4,4,64,128]{3,2,1,0:T(8,128)(2,1)S(1)} %bitcast.76), channel_id=1, source_target_pairs={{0,8},{1,17},{2,10},{3,19},{4,12},{5,21},{6,14},{7,23},{8,0},{9,25... | collective-permute-start | bytes 786440 | tf_op jit(solution)/shard_map/cond/branch_1_fun/ppermute | solution.py:335
  152.4 16.9 %collective-permute-start.18 = (bf16[4,4,64,128]{3,2,1,0:T(8,128)(2,1)S(1)}, bf16[4,4,64,128]{3,2,1,0:T(8,128)(2,1)S(1)}, u32[]{:S(2)}, u32[]{:S(2)}) collective-permute-start(bf16[4,4,64,128]{3,2,1,0:T(8,128)(2,1)S(1)} %bitcast.73), channel_id=1, source_target_pairs={{0,8},{1,17},{2,10},{3,19},{4,12},{5,21},{6,14},{7,23},{8,0},{9,25... | collective-permute-start | bytes 786440 | tf_op jit(solution)/shard_map/cond/branch_1_fun/ppermute | solution.py:335
  (2 other events, 1.9 us)
